TPU v7x, 512 devices: a whole 4x4x16 slice. The times are simulated.
512 devices in a mesh: tm: 4 (over z_lo), height: 16 (over y, z_hi), replica: 8 (over x, core).
Axes of the slice: x: 4, y: 4, z: 16 (z_hi: 4, z_lo: 4; z = z_hi * 4 + z_lo), core: 2. Of those that a mesh axis runs over, the one named last changes fastest.
Arguments:
- queries: bfloat16 [8, 16, 32, 16, 256], P('replica', 'tm', 'height'), may hold values from -16 to 16
- keys: bfloat16 [8, 16, 32, 16, 256], P('replica', 'tm', 'height'), may hold values from -16 to 16
- values: bfloat16 [8, 16, 32, 16, 256], P('replica', 'tm', 'height'), may hold values from -4 to 4
- window: int32 [2, 6], replicated, may hold values from 0 to 1, as said below
- out_weight: bfloat16 [256, 3072], replicated, may hold values from -0.375 to 0.375
- out_grad: bfloat16 [8, 16, 32, 16, 3072], P('replica', 'tm', 'height'), may hold values from -6 to 6
Outputs:
- query_grad: bfloat16 [8, 16, 32, 16, 256], P('replica', 'tm', 'height')
- key_grad: bfloat16 [8, 16, 32, 16, 256], P('replica', 'tm', 'height')
- value_grad: bfloat16 [8, 16, 32, 16, 256], P('replica', 'tm', 'height')
- weight_grad: float32 [256, 3072], P(None, 'replica')
Inputs may be any that keep to these rules, and one draw needn't show every extreme that they name: `window`: some head reaches one tile in all six directions.
All inputs are finite; a program needn't handle non-finite values.
Results may differ from a plain program's by a relative error of at most 0.035.
Values may be sent and summed in bfloat16 or wider, within the bound.
No kernel may reach another device: no remote copies, remote signals or barrier semaphores. Data moves between devices by JAX's collectives and lax.ppermute only.
A program may use at most 128 MiB of HBM per device.

v0:
```python
import jax
import jax.numpy as jnp
from jax import lax
from jax.experimental import pallas as pl
from jax.experimental.pallas import tpu as pltpu
from jax.sharding import Mesh
from jax.sharding import PartitionSpec as P

TILES = 4
HEADS = 2
HD = 128
TOK = 128
REPLICAS = 8
SLICE = 384
HIDDEN = -1e30
SCALE = HD**-0.5
F32 = jnp.float32
BF16 = jnp.bfloat16
VM = pl.BlockSpec(memory_space=pltpu.VMEM)
ANY = pl.BlockSpec(memory_space=pl.ANY)
SMEM = pl.BlockSpec(memory_space=pltpu.SMEM)
PARAMS = pltpu.CompilerParams(vmem_limit_bytes=48 * 1024 * 1024)


def dot(a, b, dim_a, dim_b):
    return lax.dot_general(a, b, (((dim_a,), (dim_b,)), ((), ())), preferred_element_type=F32)


def cost(flops, moved):
    return pl.CostEstimate(flops=flops, bytes_accessed=moved, transcendentals=0)


def shape(dims, kind=BF16):
    return jax.ShapeDtypeStruct(dims, kind)


def my_head():
    return lax.rem(lax.axis_index("zh"), HEADS)


def pack_kernel(k_ref, v_ref, kv_ref):
    for peer in range(4):
        cols = slice((peer % HEADS) * HD, (peer % HEADS + 1) * HD)
        kv_ref[peer, 0] = k_ref[:, cols]
        kv_ref[peer, 1] = v_ref[:, cols]


def project_kernel(q_ref, g_ref, w_ref, keep_ref, send_ref, part_ref):
    grad = dot(g_ref[...], w_ref[...], 1, 1).astype(BF16)
    for replica in range(REPLICAS):
        part_ref[replica] = g_ref[:, replica * SLICE : (replica + 1) * SLICE]
    head = my_head()

    def split(first, second):
        for ref, cols in ((keep_ref, first), (send_ref, second)):
            ref[0] = q_ref[:, cols]
            ref[1] = grad[:, cols]

    low, high = slice(0, HD), slice(HD, 2 * HD)

    @pl.when(head == 0)
    def _():
        split(low, high)

    @pl.when(head == 1)
    def _():
        split(high, low)


def attention_kernel(
    win_ref, own_ref, other_ref, lo_ref, mid_ref, hi_ref,
    keep_ref, send_ref, glo_ref, gmid_ref, ghi_ref,
    q_s, do_s, kv_s, g_s, score_s, bias_s, sem_in, sem_out,
):
    head = my_head()
    tile_t = lax.axis_index("tm")
    tile_y = lax.axis_index("y")
    fetches = [
        pltpu.make_async_copy(src, kv_s.at[pl.ds(3 * i, 3)], sem_in.at[i])
        for i, src in enumerate((lo_ref, mid_ref, hi_ref))
    ]
    for fetch in fetches:
        fetch.start()
    q_s[0:TOK] = own_ref[0]
    q_s[TOK : 2 * TOK] = other_ref[0]
    do_s[0:TOK] = own_ref[1]
    do_s[TOK : 2 * TOK] = other_ref[1]
    key_col = lax.broadcasted_iota(jnp.int32, bias_s.shape, 0)
    query_col = lax.broadcasted_iota(jnp.int32, bias_s.shape, 1)
    step = ((key_col >> 3) & 1) - ((query_col >> 3) & 1)
    column_ok = (step >= -win_ref[head, 4]) & (step <= win_ref[head, 5])
    bias_s[...] = jnp.where(column_ok, 0.0, HIDDEN)
    for fetch in fetches:
        fetch.wait()
    q = q_s[...]
    do = do_s[...]

    def tile_bias(b):
        dy = b // 3 - 1
        dt = b % 3 - 1
        near = (dt >= -win_ref[head, 0]) & (dt <= win_ref[head, 1])
        near &= (dy >= -win_ref[head, 2]) & (dy <= win_ref[head, 3])
        near &= (tile_t + dt >= 0) & (tile_t + dt < TILES)
        near &= (tile_y + dy >= 0) & (tile_y + dy < TILES)
        return jnp.where(near, 0.0, HIDDEN)

    def block(b, which):
        return kv_s[b, :, which].reshape(4 * TOK, HD)

    def place(b, which, grad):
        g_s[b, :, which] = grad.astype(BF16).reshape(4, TOK, HD)

    row = (1, 2 * TOK)

    def score_step(b, top):
        score = dot(block(b, 0), q, 1, 1) * SCALE + (bias_s[...] + tile_bias(b))
        score_s[b] = score
        return jnp.maximum(top, jnp.max(score, axis=0, keepdims=True))

    top = lax.fori_loop(0, 9, score_step, jnp.full(row, 2 * HIDDEN, F32))

    def sum_step(b, total):
        weight = jnp.exp(score_s[b] - top)
        score_s[b] = weight
        return total + jnp.sum(weight, axis=0, keepdims=True)

    inverse = 1.0 / lax.fori_loop(0, 9, sum_step, jnp.zeros(row, F32))

    def value_step(b, total):
        prob = score_s[b] * inverse
        score_s[b] = prob
        low = prob.astype(BF16)
        place(b, 1, dot(low, do, 1, 0))
        return total + dot(block(b, 1), low, 0, 0)

    attended = lax.fori_loop(0, 9, value_step, jnp.zeros((HD, 2 * TOK), F32))
    attended = attended.astype(BF16).astype(F32)
    grad_dot = jnp.sum(attended * do.astype(F32).T, axis=0, keepdims=True)
    attention = attended.T.astype(BF16)
    keep_ref[0] = attention[:TOK]
    send_ref[0] = attention[TOK:]

    def grad_step(b, total):
        prob_grad = dot(block(b, 1), do, 1, 1)
        low = (score_s[b] * (prob_grad - grad_dot)).astype(BF16)
        place(b, 0, dot(low, q, 1, 0) * SCALE)
        return total + dot(low, block(b, 0), 0, 0)

    query_grad = lax.fori_loop(0, 9, grad_step, jnp.zeros((2 * TOK, HD), F32))
    query_grad = (query_grad * SCALE).astype(BF16)
    keep_ref[1] = query_grad[:TOK]
    send_ref[1] = query_grad[TOK:]
    stores = [
        pltpu.make_async_copy(g_s.at[pl.ds(3 * i, 3)], dst, sem_out.at[i])
        for i, dst in enumerate((glo_ref, gmid_ref, ghi_ref))
    ]
    for store in stores:
        store.start()
    for store in stores:
        store.wait()


def row_sum_kernel(mid_ref, low_ref, high_ref, before_ref, own_ref, after_ref):
    for i, ref in enumerate((before_ref, own_ref, after_ref)):
        total = mid_ref[i].astype(F32) + low_ref[i].astype(F32) + high_ref[i].astype(F32)
        ref[...] = total.astype(BF16)


def weight_kernel(att_ref, grad_ref, out_ref):
    head = my_head()
    grad = grad_ref[...].reshape(REPLICAS * TOK, SLICE)
    for half in range(2):
        att = att_ref[:, half].reshape(REPLICAS * TOK, HD)
        term = dot(att, grad, 0, 0).astype(BF16)
        first = 8 * (head if half == 0 else 1 - head)
        for j in range(8):
            for c in range(3):
                piece = term[16 * j : 16 * (j + 1), HD * c : HD * (c + 1)]
                out_ref[first + j, 16 * c : 16 * (c + 1), :] = piece


def tile_sum_kernel(own_ref, low_ref, high_ref, weight_ref, out_ref):
    weight = weight_ref[0].astype(F32)
    for i in range(1, 16):
        weight = weight + weight_ref[i].astype(F32)
    weight = weight.astype(BF16)
    for peer in range(4):
        total = own_ref[peer].astype(F32) + low_ref[peer].astype(F32) + high_ref[peer].astype(F32)
        out_ref[peer, 0 : 2 * TOK] = total.astype(BF16).reshape(2 * TOK, HD)
        out_ref[peer, 2 * TOK :] = weight


def finish_kernel(parts_ref, own_ref, other_ref, dq_ref, dk_ref, dv_ref, weight_ref):
    for which, ref in enumerate((dk_ref, dv_ref)):
        rows = slice(which * TOK, (which + 1) * TOK)
        for head in range(HEADS):
            total = parts_ref[head, rows].astype(F32) + parts_ref[head + 2, rows].astype(F32)
            ref[:, head * HD : (head + 1) * HD] = total.astype(BF16)
    head = my_head()

    @pl.when(head == 0)
    def _():
        dq_ref[:, 0:HD] = own_ref[1]
        dq_ref[:, HD : 2 * HD] = other_ref[1]

    @pl.when(head == 1)
    def _():
        dq_ref[:, 0:HD] = other_ref[1]
        dq_ref[:, HD : 2 * HD] = own_ref[1]

    weight = parts_ref[0, 2 * TOK :].astype(F32)
    for peer in range(1, 4):
        weight = weight + parts_ref[peer, 2 * TOK :].astype(F32)
    weight = weight.astype(BF16)
    for i in range(16):
        weight_ref[i] = weight


def unpack_kernel(parts_ref, out_ref):
    for j in range(16):
        for c in range(3):
            piece = parts_ref[j, 16 * c : 16 * (c + 1), :].astype(F32)
            out_ref[16 * j : 16 * (j + 1), HD * c : HD * (c + 1)] = piece


def call(kernel, outs, count, name, **more):
    return pl.pallas_call(
        kernel,
        out_shape=outs,
        in_specs=[VM] * count,
        out_specs=jax.tree.map(lambda _: VM, outs),
        compiler_params=PARAMS,
        name=name,
        **more,
    )


def neighbours(low_block, high_block, axis):
    up = [(i, i + 1) for i in range(TILES - 1)]
    down = [(i + 1, i) for i in range(TILES - 1)]
    return lax.ppermute(high_block, axis, up), lax.ppermute(low_block, axis, down)


def exchange(block, axes):
    return lax.all_to_all(block, axes, 0, 0, tiled=True)


def on_device(queries, keys, values, window, out_weight, out_grad):
    local = queries.shape
    width = HEADS * HD
    q = queries.reshape(TOK, width)
    k = keys.reshape(TOK, width)
    v = values.reshape(TOK, width)
    g = out_grad.reshape(TOK, REPLICAS * SLICE)
    replica = ("x", "core")
    tile = ("tm", "y")
    swap = [(i, i ^ 1) for i in range(4)]

    kv = call(pack_kernel, shape((4, 2, TOK, HD)), 2, "pack")(k, v)
    own_kv = exchange(kv, "zh")
    keep, send, grad_parts = call(
        project_kernel,
        (shape((2, TOK, HD)), shape((2, TOK, HD)), shape((REPLICAS, TOK, SLICE))),
        3,
        "project",
        cost_estimate=cost(2 * TOK * width * REPLICAS * SLICE, 4 * 2**20),
    )(q, g, out_weight)
    other = lax.ppermute(send, "zh", swap)
    kv_low, kv_high = neighbours(own_kv, own_kv, "tm")
    rows_kv = jnp.stack([kv_low, own_kv, kv_high])
    rows_low, rows_high = neighbours(rows_kv, rows_kv, "y")
    grad_slices = exchange(grad_parts, replica)

    three = (3, 4, 2, TOK, HD)
    mine, theirs, grad_low, grad_mid, grad_high = pl.pallas_call(
        attention_kernel,
        out_shape=(shape((2, TOK, HD)), shape((2, TOK, HD)), shape(three), shape(three), shape(three)),
        in_specs=[SMEM, VM, VM, ANY, ANY, ANY],
        out_specs=(VM, VM, ANY, ANY, ANY),
        scratch_shapes=[
            pltpu.VMEM((2 * TOK, HD), BF16),
            pltpu.VMEM((2 * TOK, HD), BF16),
            pltpu.VMEM((9, 4, 2, TOK, HD), BF16),
            pltpu.VMEM((9, 4, 2, TOK, HD), BF16),
            pltpu.VMEM((9, 4 * TOK, 2 * TOK), F32),
            pltpu.VMEM((4 * TOK, 2 * TOK), F32),
            pltpu.SemaphoreType.DMA((3,)),
            pltpu.SemaphoreType.DMA((3,)),
        ],
        compiler_params=PARAMS,
        name="attention",
        cost_estimate=cost(7 * 2 * 9 * 4 * TOK * 2 * TOK * HD, 6 * 2**20),
    )(window, keep, other, rows_low, rows_kv, rows_high)
    partner = lax.ppermute(theirs, "zh", swap)
    from_low, from_high = neighbours(grad_low, grad_high, "y")

    att = jnp.stack([mine[0], partner[0]])
    att_all = lax.all_gather(att, replica)
    weight = call(
        weight_kernel,
        shape((16, 48, HD)),
        2,
        "weight",
        cost_estimate=cost(2 * width * REPLICAS * TOK * SLICE, 2 * 2**20),
    )(att_all, grad_slices)
    weight = exchange(weight, tile)

    before, own, after = call(row_sum_kernel, (shape((4, 2, TOK, HD)),) * 3, 3, "row_sum")(
        grad_mid, from_low, from_high
    )
    from_before, from_after = neighbours(before, after, "tm")
    parts = call(tile_sum_kernel, shape((4, 2 * TOK + 48, HD)), 4, "tile_sum")(
        own, from_before, from_after, weight
    )
    parts = exchange(parts, "zh")
    dq, dk, dv, weight = call(
        finish_kernel,
        (shape((TOK, width)),) * 3 + (shape((16, 48, HD)),),
        3,
        "finish",
    )(parts, mine, partner)
    weight = exchange(weight, tile)
    weight = call(unpack_kernel, shape((width, SLICE), F32), 1, "unpack")(weight)
    return dq.reshape(local), dk.reshape(local), dv.reshape(local), weight


def solution(mesh):
    fine = Mesh(mesh.devices.reshape(4, 4, 4, 4, 2), ("tm", "y", "zh", "x", "core"))
    tokens = P(("x", "core"), "tm", ("y", "zh"), None, None)
    return jax.shard_map(
        on_device,
        mesh=fine,
        in_specs=(tokens, tokens, tokens, P(), P(), tokens),
        out_specs=(tokens, tokens, tokens, P(None, ("x", "core"))),
        check_vma=False,
    )
```

profile of v0, /device:TPU:2, one launch (start us, length us, event | category | flops | bytes accessed | tf_op | source)
XLA Modules:
  0.0 179.6 jit_solution(16834695892301209022)
XLA Ops:
  2.5 33.6 %all_to_all.25 = bf16[4,2,128,128]{3,2,1,0:T(8,128)(2,1)S(1)} all-to-all(bf16[4,2,128,128]{3,2,1,0:T(8,128)(2,1)S(1)} %pack.1), channel_id=1, replica_groups=mesh['tm'=4,'y'=4,'zh'=4,'x'=4,'core'=2] {'zh'}, dimensions={0} | all-to-all | bytes 524288 | tf_op jit(solution)/shard_map/all_to_all | solution.py:245
  36.1 1.3 collective-permute-start.2
  37.4 6.1 %collective-permute-start.1 = (bf16[4,2,128,128]{3,2,1,0:T(8,128)(2,1)S(1)}, bf16[4,2,128,128]{3,2,1,0:T(8,128)(2,1)S(1)}, u32[]{:S(2)}, u32[]{:S(2)}) collective-permute-start(bf16[4,2,128,128]{3,2,1,0:T(8,128)(2,1)S(1)} %all_to_all.25), channel_id=1, source_target_pairs={{0,128},{128,256},{256,384},{1,129},{129,257},{257,385},{2,130},{1... | collective-permute-start | bytes 786440 | tf_op jit(solution)/shard_map/ppermute | solution.py:241
  43.6 3.1 %collective-permute-done.2 = bf16[4,2,128,128]{3,2,1,0:T(8,128)(2,1)S(1)} collective-permute-done((bf16[4,2,128,128]{3,2,1,0:T(8,128)(2,1)S(1)}, bf16[4,2,128,128]{3,2,1,0:T(8,128)(2,1)S(1)}, u32[]{:S(2)}, u32[]{:S(2)}) %collective-permute-start.2) | collective-permute-done | bytes 262176 | tf_op jit(solution)/shard_map/ppermute | solution.py:241
  48.0 1.3 collective-permute-start.4
  49.3 4.6 %collective-permute-start.3 = (bf16[3,4,2,128,128]{4,3,2,1,0:T(8,128)(2,1)S(1)}, bf16[3,4,2,128,128]{4,3,2,1,0:T(8,128)(2,1)S(1)}, u32[]{:S(2)}, u32[]{:S(2)}) collective-permute-start(bf16[3,4,2,128,128]{4,3,2,1,0:T(8,128)(2,1)S(1)} %pad_maximum_fusion.mid_ref), channel_id=1, source_target_pairs={{0,32},{32,64},{64,96},{1,33},{33,65},{65,97},{2,34},{34,66},{66,9... | collective-permute-start | bytes 2359304 | tf_op jit(solution)/shard_map/ppermute | solution.py:241
  53.9 1.5 project.1
  55.4 4.8 %all-to-all-start.1 = ((bf16[8,128,384]{2,1,0:T(8,128)(2,1)}), bf16[8,128,384]{2,1,0:T(8,128)(2,1)S(1)}, u32[]{:S(2)}, u32[]{:S(2)}) async-start(bf16[8,128,384]{2,1,0:T(8,128)(2,1)} %get-tuple-element.29), calls=%async_computation.1 | async-start | bytes 1572864 | tf_op jit(solution)/shard_map/all_to_all | solution.py:245
  60.3 4.2 %collective-permute-start = (bf16[2,128,128]{2,1,0:T(8,128)(2,1)S(1)}, bf16[2,128,128]{2,1,0:T(8,128)(2,1)S(1)}, u32[]{:S(2)}, u32[]{:S(2)}) collective-permute-start(bf16[2,128,128]{2,1,0:T(8,128)(2,1)S(1)} %get-tuple-element.20), channel_id=1, source_target_pairs={{0,8},{8,0},{16,24},{24,16},{1,9},{9,1},{17,25},{25,17},{2,10},{10... | collective-permute-start | bytes 196616 | tf_op jit(solution)/shard_map/ppermute | solution.py:268
  64.5 5.8 %collective-permute-done.other_ref = bf16[2,128,128]{2,1,0:T(8,128)(2,1)S(1)} collective-permute-done((bf16[2,128,128]{2,1,0:T(8,128)(2,1)S(1)}, bf16[2,128,128]{2,1,0:T(8,128)(2,1)S(1)}, u32[]{:S(2)}, u32[]{:S(2)}) %collective-permute-start) | collective-permute-done | bytes 65568 | tf_op jit(solution)/shard_map/ppermute | solution.py:268
  72.4 12.4 %attention.1 = (bf16[2,128,128]{2,1,0:T(8,128)(2,1)S(1)}, bf16[2,128,128]{2,1,0:T(8,128)(2,1)S(1)}, bf16[3,4,2,128,128]{4,3,2,1,0:T(8,128)(2,1)}, bf16[3,4,2,128...) custom-call(s32[2,6]{1,0:T(2,128)S(1)} %copy-done.7, bf16[2,128,128]{2,1,0:T(8,128)(2,1)S(1)} %get-tuple-element.19.own_ref, ...), custom_call_target="tpu_custom_call" | custom-call | flops 2113929216 | bytes 6291456 | tf_op jit(solution)/shard_map/attention/pallas_call | solution.py:275
  84.8 4.3 %collective-permute-start.9 = (bf16[2,128,128]{2,1,0:T(8,128)(2,1)S(1)}, bf16[2,128,128]{2,1,0:T(8,128)(2,1)S(1)}, u32[]{:S(2)}, u32[]{:S(2)}) collective-permute-start(bf16[2,128,128]{2,1,0:T(8,128)(2,1)S(1)} %get-tuple-element.28), channel_id=1, source_target_pairs={{0,8},{8,0},{16,24},{24,16},{1,9},{9,1},{17,25},{25,17},{2,10},{10... | collective-permute-start | bytes 196616 | tf_op jit(solution)/shard_map/ppermute | solution.py:294
  89.1 3.5 %collective-permute-start.5 = (bf16[3,4,2,128,128]{4,3,2,1,0:T(8,128)(2,1)}, bf16[3,4,2,128,128]{4,3,2,1,0:T(8,128)(2,1)S(1)}, u32[]{:S(2)}, u32[]{:S(2)}) collective-permute-start(bf16[3,4,2,128,128]{4,3,2,1,0:T(8,128)(2,1)} %get-tuple-element.22), channel_id=1, source_target_pairs={{0,32},{32,64},{64,96},{1,33},{33,65},{65,97},{2,34},{34,66},{66,9... | collective-permute-start | bytes 2359304 | tf_op jit(solution)/shard_map/ppermute | solution.py:241
  92.6 1.3 collective-permute-start.6
  93.9 2.3 %collective-permute-done.9.other_ref = bf16[2,128,128]{2,1,0:T(8,128)(2,1)S(1)} collective-permute-done((bf16[2,128,128]{2,1,0:T(8,128)(2,1)S(1)}, bf16[2,128,128]{2,1,0:T(8,128)(2,1)S(1)}, u32[]{:S(2)}, u32[]{:S(2)}) %collective-permute-start.9) | collective-permute-done | bytes 65568 | tf_op jit(solution)/shard_map/ppermute | solution.py:294
  96.2 13.1 %all-gather = bf16[16,128,128]{2,1,0:T(8,128)(2,1)S(1)} all-gather(bf16[2,128,128]{2,1,0:T(8,128)(2,1)S(1)} %pad_maximum_fusion.1), channel_id=2, replica_groups=mesh['tm'=4,'y'=4,'zh'=4,'x'=4,'core'=2] {'x','core'}, dimensions={0}, use_global_device_ids=true | all-gather | bytes 589824 | tf_op jit(solution)/shard_map/all_gather | solution.py:298
  110.5 10.1 %all-to-all-start.2 = ((bf16[16,48,128]{2,1,0:T(8,128)(2,1)}), bf16[16,48,128]{2,1,0:T(8,128)(2,1)S(1)}, u32[]{:S(2)}, u32[]{:S(2)}) async-start(bf16[16,48,128]{2,1,0:T(8,128)(2,1)} %weight.1), calls=%async_computation.2 | async-start | bytes 393216 | tf_op jit(solution)/shard_map/all_to_all | solution.py:245
  120.6 1.4 row_sum.1
  122.0 3.8 %collective-permute-start.7 = (bf16[4,2,128,128]{3,2,1,0:T(8,128)(2,1)S(1)}, bf16[4,2,128,128]{3,2,1,0:T(8,128)(2,1)S(1)}, u32[]{:S(2)}, u32[]{:S(2)}) collective-permute-start(bf16[4,2,128,128]{3,2,1,0:T(8,128)(2,1)S(1)} %get-tuple-element.25), channel_id=1, source_target_pairs={{0,128},{128,256},{256,384},{1,129},{129,257},{257,385},{2,130},{1... | collective-permute-start | bytes 786440 | tf_op jit(solution)/shard_map/ppermute | solution.py:241
  125.9 1.3 collective-permute-start.8
  127.2 3.5 %all-to-all-done.2.weight_ref = bf16[16,48,128]{2,1,0:T(8,128)(2,1)S(1)} async-done(((bf16[16,48,128]{2,1,0:T(8,128)(2,1)}), bf16[16,48,128]{2,1,0:T(8,128)(2,1)S(1)}, u32[]{:S(2)}, u32[]{:S(2)}) %all-to-all-start.2) | async-done | bytes 196640 | tf_op jit(solution)/shard_map/all_to_all | solution.py:245
  131.4 4.1 %collective-permute-done.8.high_ref = bf16[4,2,128,128]{3,2,1,0:T(8,128)(2,1)S(1)} collective-permute-done((bf16[4,2,128,128]{3,2,1,0:T(8,128)(2,1)S(1)}, bf16[4,2,128,128]{3,2,1,0:T(8,128)(2,1)S(1)}, u32[]{:S(2)}, u32[]{:S(2)}) %collective-permute-start.8) | collective-permute-done | bytes 262176 | tf_op jit(solution)/shard_map/ppermute | solution.py:241
  135.6 23.4 %all_to_all.26.parts_ref = bf16[4,304,128]{2,1,0:T(8,128)(2,1)S(1)} all-to-all(bf16[4,304,128]{2,1,0:T(8,128)(2,1)S(1)} %tile_sum.1), channel_id=1, replica_groups=mesh['tm'=4,'y'=4,'zh'=4,'x'=4,'core'=2] {'zh'}, dimensions={0} | all-to-all | bytes 622592 | tf_op jit(solution)/shard_map/all_to_all | solution.py:245
  159.7 19.1 %all_to_all.27.parts_ref = bf16[16,48,128]{2,1,0:T(8,128)(2,1)S(1)} all-to-all(bf16[16,48,128]{2,1,0:T(8,128)(2,1)S(1)} %get-tuple-element.33), channel_id=1, replica_groups=mesh['tm'=4,'y'=4,'zh'=4,'x'=4,'core'=2] {'tm','y'}, dimensions={0} | all-to-all | bytes 393216 | tf_op jit(solution)/shard_map/all_to_all | solution.py:245
  (32 shorter events, 8.6 us)
Async XLA Ops:
  0.6 53.2 %copy-start.1 = (bf16[1,4,2,16,3072]{4,3,2,1,0:T(8,128)(2,1)S(1)}, bf16[1,4,2,16,3072]{4,3,2,1,0:T(8,128)(2,1)}, u32[]{:S(2)}) copy-start(bf16[1,4,2,16,3072]{4,3,2,1,0:T(8,128)(2,1)} %param.11) | copy-start | bytes 2359300
  0.6 53.2 %copy-start = (bf16[256,3072]{1,0:T(8,128)(2,1)S(1)}, bf16[256,3072]{1,0:T(8,128)(2,1)}, u32[]{:S(2)}) copy-start(bf16[256,3072]{1,0:T(8,128)(2,1)} %w_ref.1) | copy-start | bytes 4718596
  0.7 53.2 %copy-start.2 = (bf16[1,4,2,16,256]{4,3,2,1,0:T(8,128)(2,1)S(1)}, bf16[1,4,2,16,256]{4,3,2,1,0:T(8,128)(2,1)}, u32[]{:S(2)}) copy-start(bf16[1,4,2,16,256]{4,3,2,1,0:T(8,128)(2,1)} %param.6) | copy-start | bytes 196612
  0.7 1.0 copy-start.3
  1.7 0.8 copy-start.4
  36.1 10.5 %collective-permute-start.2 = (bf16[4,2,128,128]{3,2,1,0:T(8,128)(2,1)S(1)}, bf16[4,2,128,128]{3,2,1,0:T(8,128)(2,1)S(1)}, u32[]{:S(2)}, u32[]{:S(2)}) collective-permute-start(bf16[4,2,128,128]{3,2,1,0:T(8,128)(2,1)S(1)} %all_to_all.25), channel_id=1, source_target_pairs={{128,0},{256,128},{384,256},{129,1},{257,129},{385,257},{130,2},{2... | collective-permute-start | bytes 786440 | tf_op jit(solution)/shard_map/ppermute | solution.py:241
  37.4 10.4 %collective-permute-start.1 = (bf16[4,2,128,128]{3,2,1,0:T(8,128)(2,1)S(1)}, bf16[4,2,128,128]{3,2,1,0:T(8,128)(2,1)S(1)}, u32[]{:S(2)}, u32[]{:S(2)}) collective-permute-start(bf16[4,2,128,128]{3,2,1,0:T(8,128)(2,1)S(1)} %all_to_all.25), channel_id=1, source_target_pairs={{0,128},{128,256},{256,384},{1,129},{129,257},{257,385},{2,130},{1... | collective-permute-start | bytes 786440 | tf_op jit(solution)/shard_map/ppermute | solution.py:241
  48.0 22.4 %collective-permute-start.4 = (bf16[3,4,2,128,128]{4,3,2,1,0:T(8,128)(2,1)S(1)}, bf16[3,4,2,128,128]{4,3,2,1,0:T(8,128)(2,1)S(1)}, u32[]{:S(2)}, u32[]{:S(2)}) collective-permute-start(bf16[3,4,2,128,128]{4,3,2,1,0:T(8,128)(2,1)S(1)} %pad_maximum_fusion.mid_ref), channel_id=1, source_target_pairs={{32,0},{64,32},{96,64},{33,1},{65,33},{97,65},{34,2},{66,34},{98,6... | collective-permute-start | bytes 2359304 | tf_op jit(solution)/shard_map/ppermute | solution.py:241
  49.3 21.1 %collective-permute-start.3 = (bf16[3,4,2,128,128]{4,3,2,1,0:T(8,128)(2,1)S(1)}, bf16[3,4,2,128,128]{4,3,2,1,0:T(8,128)(2,1)S(1)}, u32[]{:S(2)}, u32[]{:S(2)}) collective-permute-start(bf16[3,4,2,128,128]{4,3,2,1,0:T(8,128)(2,1)S(1)} %pad_maximum_fusion.mid_ref), channel_id=1, source_target_pairs={{0,32},{32,64},{64,96},{1,33},{33,65},{65,97},{2,34},{34,66},{66,9... | collective-permute-start | bytes 2359304 | tf_op jit(solution)/shard_map/ppermute | solution.py:241
  53.9 17.4 %copy-start.7 = (s32[2,6]{1,0:T(2,128)S(1)}, s32[2,6]{1,0:T(2,128)}, u32[]{:S(2)}) copy-start(s32[2,6]{1,0:T(2,128)} %win_ref.1) | copy-start | bytes 148
  55.4 53.9 %all-to-all-start.1 = ((bf16[8,128,384]{2,1,0:T(8,128)(2,1)}), bf16[8,128,384]{2,1,0:T(8,128)(2,1)S(1)}, u32[]{:S(2)}, u32[]{:S(2)}) async-start(bf16[8,128,384]{2,1,0:T(8,128)(2,1)} %get-tuple-element.29), calls=%async_computation.1 | async-start | bytes 1572864 | tf_op jit(solution)/shard_map/all_to_all | solution.py:245
  60.3 10.1 %collective-permute-start = (bf16[2,128,128]{2,1,0:T(8,128)(2,1)S(1)}, bf16[2,128,128]{2,1,0:T(8,128)(2,1)S(1)}, u32[]{:S(2)}, u32[]{:S(2)}) collective-permute-start(bf16[2,128,128]{2,1,0:T(8,128)(2,1)S(1)} %get-tuple-element.20), channel_id=1, source_target_pairs={{0,8},{8,0},{16,24},{24,16},{1,9},{9,1},{17,25},{25,17},{2,10},{10... | collective-permute-start | bytes 196616 | tf_op jit(solution)/shard_map/ppermute | solution.py:268
  70.3 0.9 copy-start.5
  71.3 1.1 copy-start.6
  84.8 11.4 %collective-permute-start.9 = (bf16[2,128,128]{2,1,0:T(8,128)(2,1)S(1)}, bf16[2,128,128]{2,1,0:T(8,128)(2,1)S(1)}, u32[]{:S(2)}, u32[]{:S(2)}) collective-permute-start(bf16[2,128,128]{2,1,0:T(8,128)(2,1)S(1)} %get-tuple-element.28), channel_id=1, source_target_pairs={{0,8},{8,0},{16,24},{24,16},{1,9},{9,1},{17,25},{25,17},{2,10},{10... | collective-permute-start | bytes 196616 | tf_op jit(solution)/shard_map/ppermute | solution.py:294
  89.1 31.5 %collective-permute-start.5 = (bf16[3,4,2,128,128]{4,3,2,1,0:T(8,128)(2,1)}, bf16[3,4,2,128,128]{4,3,2,1,0:T(8,128)(2,1)S(1)}, u32[]{:S(2)}, u32[]{:S(2)}) collective-permute-start(bf16[3,4,2,128,128]{4,3,2,1,0:T(8,128)(2,1)} %get-tuple-element.22), channel_id=1, source_target_pairs={{0,32},{32,64},{64,96},{1,33},{33,65},{65,97},{2,34},{34,66},{66,9... | collective-permute-start | bytes 2359304 | tf_op jit(solution)/shard_map/ppermute | solution.py:241
  92.6 28.0 %collective-permute-start.6 = (bf16[3,4,2,128,128]{4,3,2,1,0:T(8,128)(2,1)}, bf16[3,4,2,128,128]{4,3,2,1,0:T(8,128)(2,1)}, u32[]{:S(2)}, u32[]{:S(2)}) collective-permute-start(bf16[3,4,2,128,128]{4,3,2,1,0:T(8,128)(2,1)} %get-tuple-element.23), channel_id=1, source_target_pairs={{32,0},{64,32},{96,64},{33,1},{65,33},{97,65},{34,2},{66,34},{98,6... | collective-permute-start | bytes 2359304 | tf_op jit(solution)/shard_map/ppermute | solution.py:241
  110.5 20.2 %all-to-all-start.2 = ((bf16[16,48,128]{2,1,0:T(8,128)(2,1)}), bf16[16,48,128]{2,1,0:T(8,128)(2,1)S(1)}, u32[]{:S(2)}, u32[]{:S(2)}) async-start(bf16[16,48,128]{2,1,0:T(8,128)(2,1)} %weight.1), calls=%async_computation.2 | async-start | bytes 393216 | tf_op jit(solution)/shard_map/all_to_all | solution.py:245
  122.0 9.3 %collective-permute-start.7 = (bf16[4,2,128,128]{3,2,1,0:T(8,128)(2,1)S(1)}, bf16[4,2,128,128]{3,2,1,0:T(8,128)(2,1)S(1)}, u32[]{:S(2)}, u32[]{:S(2)}) collective-permute-start(bf16[4,2,128,128]{3,2,1,0:T(8,128)(2,1)S(1)} %get-tuple-element.25), channel_id=1, source_target_pairs={{0,128},{128,256},{256,384},{1,129},{129,257},{257,385},{2,130},{1... | collective-permute-start | bytes 786440 | tf_op jit(solution)/shard_map/ppermute | solution.py:241
  125.9 9.6 %collective-permute-start.8 = (bf16[4,2,128,128]{3,2,1,0:T(8,128)(2,1)S(1)}, bf16[4,2,128,128]{3,2,1,0:T(8,128)(2,1)S(1)}, u32[]{:S(2)}, u32[]{:S(2)}) collective-permute-start(bf16[4,2,128,128]{3,2,1,0:T(8,128)(2,1)S(1)} %get-tuple-element.26), channel_id=1, source_target_pairs={{128,0},{256,128},{384,256},{129,1},{257,129},{385,257},{130,2},{2... | collective-permute-start | bytes 786440 | tf_op jit(solution)/shard_map/ppermute | solution.py:241
where the time goes:
time: 180 us
  blocking collectives  89.2 us (50%)
  starting transfers between devices  46.7 us (26%)
  waiting for transfers between devices  20.7 us (12%)
  Pallas kernels  18.1 us (10%)
  local copies, waits for them, and re-layouts  3.91 us (2%)
    all_to_all x3, blocking collectives, exchange(): return lax.all_to_all(block, axes, 0, 0, tiled=True)  76.1 us
    ppermute x4, starting transfers between devices, neighbours(): lax.ppermute(high_block, axis, up)  18.1 us
    all_to_all x2, starting transfers between devices, exchange(): return lax.all_to_all(block, axes, 0, 0, tiled=True)  14.9 us
    all_gather x1, blocking collectives, on_device(): att_all = lax.all_gather(att, replica)  13.1 us
    pallas_call x1, Pallas kernels, on_device(): pl.pallas_call(attention_kernel, out_shape=(shape((2, TOK, HD)), shape((2...  12.4 us
    ppermute x4, waiting for transfers between devices, neighbours(): lax.ppermute(low_block, axis, down)  7.26 us
    ppermute x1, waiting for transfers between devices, on_device(): other = lax.ppermute(send, 'zh', swap)  5.83 us
    ppermute x4, starting transfers between devices, neighbours(): lax.ppermute(low_block, axis, down)  5.16 us
  transfers between devices with their start and end apart: 12, of which 7 were waited for; matrix products, arithmetic and copies ran while one was open for 0% of the time, Pallas kernels for 9%

commit v1 on v0

v1 whole, which is shorter than its diff:
```python
import jax
import jax.numpy as jnp
from jax import lax
from jax.experimental import pallas as pl
from jax.experimental.pallas import tpu as pltpu
from jax.sharding import Mesh
from jax.sharding import PartitionSpec as P

TILES = 4
SLABS = 4
HEADS = 2
HD = 128
TOK = 128
WIDTH = HEADS * HD
QUERIES = SLABS * TOK
REPLICAS = 8
SLICE = 384
HIDDEN = -1e30
SCALE = HD**-0.5
LOG2E = 1.4426950408889634
F32 = jnp.float32
BF16 = jnp.bfloat16
VM = pl.BlockSpec(memory_space=pltpu.VMEM)
SMEM = pl.BlockSpec(memory_space=pltpu.SMEM)


def dot(a, b, dim_a, dim_b):
    return lax.dot_general(a, b, (((dim_a,), (dim_b,)), ((), ())), preferred_element_type=F32)


def shape(dims, kind=BF16):
    return jax.ShapeDtypeStruct(dims, kind)


def columns(head):
    return slice(head * HD, (head + 1) * HD)


def project_kernel(q_ref, g_ref, w_ref, out_ref, part_ref):
    out_ref[0] = q_ref[...]
    out_ref[1] = dot(g_ref[...], w_ref[...], 1, 1).astype(BF16)
    for replica in range(REPLICAS):
        part_ref[replica] = g_ref[:, replica * SLICE : (replica + 1) * SLICE]


def row_bias(win_ref, head, dy):
    tile_t = lax.axis_index("tm")
    tile_y = lax.axis_index("y")
    dims = (2, 8, QUERIES)
    key_tile = lax.broadcasted_iota(jnp.int32, dims, 0)
    query_tile = (lax.broadcasted_iota(jnp.int32, dims, 2) >> 3) & 1
    step = key_tile - query_tile
    bias = jnp.where((step >= -win_ref[head, 4]) & (step <= win_ref[head, 5]), 0.0, HIDDEN)
    row_ok = (dy >= -win_ref[head, 2]) & (dy <= win_ref[head, 3])
    row_ok &= (tile_y + dy >= 0) & (tile_y + dy < TILES)
    parts = []
    for dt in (-1, 0, 1):
        ok = row_ok & (dt >= -win_ref[head, 0]) & (dt <= win_ref[head, 1])
        ok &= (tile_t + dt >= 0) & (tile_t + dt < TILES)
        parts.append(bias + jnp.where(ok, 0.0, HIDDEN))
    return jnp.stack(parts)


def hidden_scores(keys, queries, bias):
    score = dot(keys, queries, 1, 1) * (SCALE * LOG2E)
    dims = score.shape
    score = score.reshape(3, TOK // 16, 2, 8, dims[1]) + bias[:, None]
    return score.reshape(dims)


def tokens_of(ref, which, head):
    block = ref[:, which, :, columns(head)]
    return block.reshape(block.shape[0] * TOK, HD)


def split3(value):
    first = value.astype(BF16).astype(F32)
    second = (value - first).astype(BF16).astype(F32)
    return [first, second, value - first - second]


def forward_kernel(win_ref, asked_ref, low_ref, own_ref, high_ref, out_ref, score_s):
    rows = []
    for head in range(HEADS):
        queries = tokens_of(asked_ref, 0, head)
        grads = tokens_of(asked_ref, 1, head)
        refs = (low_ref, own_ref, high_ref)
        top = None
        for i, ref in enumerate(refs):
            score = hidden_scores(
                tokens_of(ref, 0, head), queries, row_bias(win_ref, head, i - 1)
            )
            score_s[i] = score
            most = jnp.max(score, axis=0, keepdims=True)
            top = most if top is None else jnp.maximum(top, most)
        total = jnp.zeros((1, QUERIES), F32)
        grad_dot = jnp.zeros((1, QUERIES), F32)
        attended = jnp.zeros((HD, QUERIES), F32)
        for i, ref in enumerate(refs):
            values = tokens_of(ref, 1, head)
            weight = jnp.exp2(score_s[i] - top)
            total = total + jnp.sum(weight, axis=0, keepdims=True)
            prob_grad = dot(values, grads, 1, 1)
            grad_dot = grad_dot + jnp.sum(weight * prob_grad, axis=0, keepdims=True)
            attended = attended + dot(values, weight.astype(BF16), 0, 0)
        inverse = 1.0 / total
        attended = (attended * inverse).astype(BF16)
        for peer in range(SLABS):
            out_ref[peer, columns(head)] = attended[:, peer * TOK : (peer + 1) * TOK]
        rows += split3(top + jnp.log2(total)) + split3(grad_dot * inverse)
    index = lax.broadcasted_iota(jnp.int32, (16, QUERIES), 0)
    stats = jnp.zeros((16, QUERIES), F32)
    for i, row in enumerate(rows):
        stats = jnp.where(index == i, row, stats)
    stats = stats.astype(BF16)
    for peer in range(SLABS):
        for slab in range(SLABS):
            first = WIDTH + 16 * slab
            out_ref[peer, first : first + 16] = stats[:, slab * TOK : (slab + 1) * TOK]


def total_stats(stats, head):
    levels, dots = [], []
    for block in stats:
        rows = [block[6 * head + i : 6 * head + i + 1] for i in range(6)]
        levels.append(rows[0] + rows[1] + rows[2])
        dots.append(rows[3] + rows[4] + rows[5])
    top = jnp.maximum(
        jnp.maximum(levels[0], levels[1]), jnp.maximum(levels[2], levels[3])
    )
    weights = [jnp.exp2(level - top) for level in levels]
    total = (weights[0] + weights[1]) + (weights[2] + weights[3])
    inverse = 1.0 / total
    weights = [weight * inverse for weight in weights]
    grad_dot = sum(weight * part for weight, part in zip(weights, dots))
    return weights, top + jnp.log2(total), grad_dot


def combine_kernel(parts_ref, out_ref):
    first = pl.multiple_of(WIDTH + 16 * lax.axis_index("zh"), 16)
    stats = [parts_ref[src, pl.ds(first, 16)].astype(F32) for src in range(SLABS)]
    for head in range(HEADS):
        weights, _, _ = total_stats(stats, head)
        attended = jnp.zeros((HD, TOK), F32)
        for src in range(SLABS):
            attended = attended + parts_ref[src, columns(head)].astype(F32) * weights[src]
        attended = attended.T.astype(BF16)
        for replica in range(REPLICAS):
            out_ref[replica, :, columns(head)] = attended


def backward_kernel(
    win_ref, asked_ref, parts_ref, low_ref, own_ref, high_ref,
    out_low_ref, out_own_ref, out_high_ref, dq_ref,
):
    stats = [
        jnp.concatenate(
            [
                parts_ref[src, WIDTH + 16 * slab : WIDTH + 16 * slab + 16].astype(F32)
                for slab in range(SLABS)
            ],
            axis=1,
        )
        for src in range(SLABS)
    ]
    pairs = ((low_ref, out_low_ref), (own_ref, out_own_ref), (high_ref, out_high_ref))
    for head in range(HEADS):
        _, level, grad_dot = total_stats(stats, head)
        queries = tokens_of(asked_ref, 0, head)
        grads = tokens_of(asked_ref, 1, head)
        query_grad = jnp.zeros((QUERIES, HD), F32)
        for i, (ref, out_ref) in enumerate(pairs):
            keys = tokens_of(ref, 0, head)
            values = tokens_of(ref, 1, head)
            score = hidden_scores(keys, queries, row_bias(win_ref, head, i - 1))
            prob = jnp.exp2(score - level)
            score_grad = (prob * (dot(values, grads, 1, 1) - grad_dot)).astype(BF16)
            value_grad = dot(prob.astype(BF16), grads, 1, 0).astype(BF16)
            key_grad = (dot(score_grad, queries, 1, 0) * SCALE).astype(BF16)
            out_ref[:, 0, :, columns(head)] = key_grad.reshape(3, TOK, HD)
            out_ref[:, 1, :, columns(head)] = value_grad.reshape(3, TOK, HD)
            query_grad = query_grad + dot(score_grad, keys, 0, 0)
        query_grad = (query_grad * SCALE).astype(BF16)
        for slab in range(SLABS):
            dq_ref[slab, columns(head)] = query_grad[slab * TOK : (slab + 1) * TOK]


def add3(a, b, c):
    return (a.astype(F32) + b.astype(F32) + c.astype(F32)).astype(BF16)


def row_sum_kernel(own_ref, low_ref, high_ref, before_ref, mid_ref, after_ref):
    for i, ref in enumerate((before_ref, mid_ref, after_ref)):
        ref[...] = add3(own_ref[i], low_ref[i], high_ref[i])


def frame_sum_kernel(own_ref, low_ref, high_ref, dk_ref, dv_ref):
    for i, ref in enumerate((dk_ref, dv_ref)):
        ref[...] = add3(own_ref[i], low_ref[i], high_ref[i])


def weight_kernel(att_ref, grad_ref, out_ref):
    att = att_ref[...].reshape(REPLICAS * TOK, WIDTH)
    grad = grad_ref[...].reshape(REPLICAS * TOK, SLICE)
    term = dot(att, grad, 0, 0).astype(BF16)
    for j in range(16):
        for c in range(3):
            piece = term[16 * j : 16 * (j + 1), HD * c : HD * (c + 1)]
            out_ref[j, 16 * c : 16 * (c + 1), :] = piece


def sum_over(ref, count, rows=slice(None)):
    total = ref[0, rows].astype(F32)
    for i in range(1, count):
        total = total + ref[i, rows].astype(F32)
    return total.astype(BF16)


def merge_kernel(dq_ref, weight_ref, out_ref):
    weight = sum_over(weight_ref, 16)
    for peer in range(SLABS):
        out_ref[peer, 0:WIDTH] = dq_ref[peer]
        out_ref[peer, WIDTH:] = weight


def weight_total_kernel(parts_ref, out_ref):
    total = sum_over(parts_ref, SLABS, slice(WIDTH, WIDTH + 48))
    for i in range(16):
        out_ref[i] = total


def query_sum_kernel(parts_ref, dq_ref):
    for head in range(HEADS):
        dq_ref[:, columns(head)] = sum_over(parts_ref, SLABS, columns(head))


def unpack_kernel(parts_ref, out_ref):
    for j in range(16):
        for c in range(3):
            piece = parts_ref[j, 16 * c : 16 * (c + 1), :].astype(F32)
            out_ref[16 * j : 16 * (j + 1), HD * c : HD * (c + 1)] = piece


def call(kernel, outs, specs, name, work=0, scratch=(), limit=4):
    return pl.pallas_call(
        kernel,
        out_shape=outs,
        in_specs=specs if isinstance(specs, list) else [VM] * specs,
        out_specs=jax.tree.map(lambda _: VM, outs),
        scratch_shapes=scratch,
        compiler_params=pltpu.CompilerParams(vmem_limit_bytes=limit * 2**20),
        cost_estimate=pl.CostEstimate(flops=work, bytes_accessed=2**20, transcendentals=0),
        name=name,
    )


def neighbours(low_block, high_block, axis):
    up = [(i, i + 1) for i in range(TILES - 1)]
    down = [(i + 1, i) for i in range(TILES - 1)]
    return lax.ppermute(high_block, axis, up), lax.ppermute(low_block, axis, down)


def after(block, *others):
    return lax.optimization_barrier((block, *others))[0]


def exchange(block, axes):
    return lax.all_to_all(block, axes, 0, 0, tiled=True)


def on_device(queries, keys, values, window, out_weight, out_grad):
    local = queries.shape
    q = queries.reshape(TOK, WIDTH)
    g = out_grad.reshape(TOK, REPLICAS * SLICE)
    replica = ("x", "core")
    tile = ("tm", "y")
    row = shape((3, 2, TOK, WIDTH))
    tokens = shape((TOK, WIDTH))
    pair_work = 2 * HEADS * QUERIES * 9 * TOK * HD

    kv = jnp.stack([keys.reshape(TOK, WIDTH), values.reshape(TOK, WIDTH)])
    kv_low, kv_high = neighbours(kv, kv, "tm")
    rows = jnp.stack([kv_low, kv, kv_high])
    rows_low, rows_high = neighbours(rows, rows, "y")
    asked, grad_parts = call(
        project_kernel,
        (shape((2, TOK, WIDTH)), shape((REPLICAS, TOK, SLICE))),
        3,
        "project",
        2 * TOK * WIDTH * REPLICAS * SLICE,
        limit=8,
    )(q, g, out_weight)
    grad_slices = exchange(grad_parts, replica)
    asked = lax.all_gather(asked, "zh")
    near = (rows_low, rows, rows_high)

    parts = call(
        forward_kernel,
        shape((SLABS, WIDTH + 16 * SLABS, HD)),
        [SMEM] + [VM] * 4,
        "forward",
        3 * pair_work,
        [pltpu.VMEM((3, 3 * TOK, QUERIES), F32)],
        10,
    )(window, asked, *near)
    parts = exchange(after(parts, grad_slices), "zh")
    att = call(combine_kernel, shape((REPLICAS, TOK, WIDTH)), 1, "combine")(parts)
    att = exchange(att, replica)
    grad_low, grad_own, grad_high, dq = call(
        backward_kernel,
        (row, row, row, shape((SLABS, WIDTH, HD))),
        [SMEM] + [VM] * 5,
        "backward",
        5 * pair_work,
        limit=10,
    )(window, asked, parts, *near)
    from_low, from_high = neighbours(grad_low, grad_high, "y")
    weight = call(
        weight_kernel,
        shape((16, 48, HD)),
        2,
        "weight",
        2 * WIDTH * REPLICAS * TOK * SLICE,
    )(after(att, grad_low), grad_slices)
    weight = exchange(weight, tile)
    before, mid, behind = call(row_sum_kernel, (shape((2, TOK, WIDTH)),) * 3, 3, "row_sum", limit=8)(
        grad_own, from_low, from_high
    )
    from_before, from_behind = neighbours(before, behind, "tm")
    dk, dv = call(frame_sum_kernel, (tokens, tokens), 3, "frame_sum")(
        mid, from_before, from_behind
    )
    merged = call(merge_kernel, shape((SLABS, WIDTH + 48, HD)), 2, "merge")(
        dq, weight
    )
    merged = exchange(merged, "zh")
    weight = call(weight_total_kernel, shape((16, 48, HD)), 1, "weight_total")(
        after(merged, from_low, from_high)
    )
    weight = exchange(weight, tile)
    dq = call(query_sum_kernel, tokens, 1, "query_sum")(merged)
    weight = call(unpack_kernel, shape((WIDTH, SLICE), F32), 1, "unpack")(
        after(weight, dq, dk, dv)
    )
    return dq.reshape(local), dk.reshape(local), dv.reshape(local), weight


def solution(mesh):
    fine = Mesh(mesh.devices.reshape(4, 4, 4, 4, 2), ("tm", "y", "zh", "x", "core"))
    tokens = P(("x", "core"), "tm", ("y", "zh"), None, None)
    return jax.shard_map(
        on_device,
        mesh=fine,
        in_specs=(tokens, tokens, tokens, P(), P(), tokens),
        out_specs=(tokens, tokens, tokens, P(None, ("x", "core"))),
        check_vma=False,
    )
```

time: 180 us -> 164 us (0.911)
  the two profiles are of different devices: /device:TPU:2 before, /device:TPU:8 now
where the time goes in v1:
time: 164 us; the launch traced here: 163 us
  blocking collectives  74.3 us (45%)
  starting transfers between devices  43.5 us (27%)
  waiting for transfers between devices  21.4 us (13%)
  Pallas kernels  13.7 us (8%)
  local copies, waits for them, and re-layouts  8.37 us (5%)
    all_to_all x2, blocking collectives, exchange(): return lax.all_to_all(block, axes, 0, 0, tiled=True)  40.7 us
    all_gather x1, blocking collectives, on_device(): asked = lax.all_gather(asked, 'zh')  33.5 us
    all_to_all x4, starting transfers between devices, exchange(): return lax.all_to_all(block, axes, 0, 0, tiled=True)  18.2 us
    ppermute x4, starting transfers between devices, neighbours(): lax.ppermute(low_block, axis, down)  13.2 us
    ppermute x4, starting transfers between devices, neighbours(): lax.ppermute(high_block, axis, up)  12.2 us
    all_to_all x4, waiting for transfers between devices, exchange(): return lax.all_to_all(block, axes, 0, 0, tiled=True)  8.69 us
    unnamed x24, local copies, waits for them, and re-layouts  8.37 us
    ppermute x4, waiting for transfers between devices, neighbours(): lax.ppermute(high_block, axis, up)  6.43 us
  transfers between devices with their start and end apart: 12, of which 6 were waited for; matrix products, arithmetic and copies ran while one was open for 0% of the time, Pallas kernels for 6%

profile of v1, /device:TPU:8, one launch (start us, length us, event | category | flops | bytes accessed | tf_op | source)
XLA Modules:
  0.0 163.0 jit_solution(886319725388522178)
XLA Ops:
  1.5 1.3 collective-permute-start.1
  2.8 4.6 %collective-permute-start = (bf16[2,128,256]{2,1,0:T(8,128)(2,1)S(1)}, bf16[2,128,256]{2,1,0:T(8,128)(2,1)S(1)}, u32[]{:S(2)}, u32[]{:S(2)}) collective-permute-start(bf16[2,128,256]{2,1,0:T(8,128)(2,1)S(1)} %get-tuple-element.35), channel_id=1, source_target_pairs={{0,128},{128,256},{256,384},{1,129},{129,257},{257,385},{2,130},{1... | collective-permute-start | bytes 393224 | tf_op jit(solution)/shard_map/ppermute | solution.py:260
  7.4 1.4 copy-done
  10.8 1.5 project.1
  12.3 4.4 %all-to-all-start = ((bf16[8,128,384]{2,1,0:T(8,128)(2,1)}), bf16[8,128,384]{2,1,0:T(8,128)(2,1)S(1)}, u32[]{:S(2)}, u32[]{:S(2)}) async-start(bf16[8,128,384]{2,1,0:T(8,128)(2,1)} %get-tuple-element.20), calls=%async_computation | async-start | bytes 1572864 | tf_op jit(solution)/shard_map/all_to_all | solution.py:268
  16.8 7.0 %collective-permute-start.3 = (bf16[3,2,128,256]{3,2,1,0:T(8,128)(2,1)S(1)}, bf16[3,2,128,256]{3,2,1,0:T(8,128)(2,1)S(1)}, u32[]{:S(2)}, u32[]{:S(2)}) collective-permute-start(bf16[3,2,128,256]{3,2,1,0:T(8,128)(2,1)S(1)} %pad_maximum_fusion.own_ref), channel_id=1, source_target_pairs={{32,0},{64,32},{96,64},{33,1},{65,33},{97,65},{34,2},{66,34},{98,6... | collective-permute-start | bytes 1179656 | tf_op jit(solution)/shard_map/ppermute | solution.py:260
  23.8 1.9 %collective-permute-start.2 = (bf16[3,2,128,256]{3,2,1,0:T(8,128)(2,1)S(1)}, bf16[3,2,128,256]{3,2,1,0:T(8,128)(2,1)S(1)}, u32[]{:S(2)}, u32[]{:S(2)}) collective-permute-start(bf16[3,2,128,256]{3,2,1,0:T(8,128)(2,1)S(1)} %pad_maximum_fusion.own_ref), channel_id=1, source_target_pairs={{0,32},{32,64},{64,96},{1,33},{33,65},{65,97},{2,34},{34,66},{66,9... | collective-permute-start | bytes 1179656 | tf_op jit(solution)/shard_map/ppermute | solution.py:260
  25.7 33.5 %all-gather = bf16[8,128,256]{2,1,0:T(8,128)(2,1)S(1)} all-gather(bf16[2,128,256]{2,1,0:T(8,128)(2,1)S(1)} %get-tuple-element.19), channel_id=2, replica_groups=mesh['tm'=4,'y'=4,'zh'=4,'x'=4,'core'=2] {'zh'}, dimensions={0}, use_global_device_ids=true | all-gather | bytes 655360 | tf_op jit(solution)/shard_map/all_gather | solution.py:294
  59.3 3.1 %forward.1 = bf16[4,320,128]{2,1,0:T(8,128)(2,1)S(1)} custom-call(s32[2,6]{1,0:T(2,128)S(1)} %copy-done.11, bf16[4,2,128,256]{3,2,1,0:T(8,128)(2,1)S(1)} %bitcast.13, bf16[3,2,128,256]{3,2,1,0:T(8,128)(2,1)S(1)} %collective-permute-done.2.low_ref, bf16[3,2,128,256]{3,2,1,0:T(8,128)(2,1)S(1)} %pad_maximum_fusion.own_ref, ...), custom_call_target="tpu_custom_call" | custom-call | flops 905969664 | bytes 1048576 | tf_op jit(solution)/shard_map/forward/pallas_call | solution.py:297
  63.9 26.4 %all_to_all.30.parts_ref = bf16[4,320,128]{2,1,0:T(8,128)(2,1)S(1)} all-to-all(bf16[4,320,128]{2,1,0:T(8,128)(2,1)S(1)} %forward.1), channel_id=1, replica_groups=mesh['tm'=4,'y'=4,'zh'=4,'x'=4,'core'=2] {'zh'}, dimensions={0} | all-to-all | bytes 655360 | tf_op jit(solution)/shard_map/all_to_all | solution.py:268
  91.3 3.5 %all-to-all-start.2 = ((bf16[8,128,256]{2,1,0:T(8,128)(2,1)}), bf16[8,128,256]{2,1,0:T(8,128)(2,1)S(1)}, u32[]{:S(2)}, u32[]{:S(2)}) async-start(bf16[8,128,256]{2,1,0:T(8,128)(2,1)} %combine.1), calls=%async_computation.2 | async-start | bytes 1048576 | tf_op jit(solution)/shard_map/all_to_all | solution.py:268
  96.8 3.9 %backward.1 = (bf16[3,2,128,256]{3,2,1,0:T(8,128)(2,1)S(1)}, bf16[3,2,128,256]{3,2,1,0:T(8,128)(2,1)S(1)}, bf16[3,2,128,256]{3,2,1,0:T(8,128)(2,1)S(1)}, bf16[4,256,128]{2,1,0:T(8,128)(2,1)S(1)}) custom-call(s32[2,6]{1,0:T(2,128)S(1)} %copy-done.11, bf16[4,2,128,256]{3,2,1,0:T(8,128)(2,1)S(1)} %bitcast.14, bf16[4,320,128]{2,1,0:T(8,128)(2,1)S(1)} %all_to_all.30.parts_ref, ...), custom_call_target="tpu_custom_call" | custom-call | flops 1509949440 | bytes 1048576 | tf_op jit(solution)/shard_map/backward/pallas_call | solution.py:309
  102.2 2.9 %all-to-all-done.2.att_ref = bf16[8,128,256]{2,1,0:T(8,128)(2,1)S(1)} async-done(((bf16[8,128,256]{2,1,0:T(8,128)(2,1)}), bf16[8,128,256]{2,1,0:T(8,128)(2,1)S(1)}, u32[]{:S(2)}, u32[]{:S(2)}) %all-to-all-start.2) | async-done | bytes 524320 | tf_op jit(solution)/shard_map/all_to_all | solution.py:268
  105.6 14.4 %all_to_all.31.weight_ref = bf16[16,48,128]{2,1,0:T(8,128)(2,1)S(1)} all-to-all(bf16[16,48,128]{2,1,0:T(8,128)(2,1)S(1)} %weight.1), channel_id=1, replica_groups=mesh['tm'=4,'y'=4,'zh'=4,'x'=4,'core'=2] {'tm','y'}, dimensions={0} | all-to-all | bytes 393216 | tf_op jit(solution)/shard_map/all_to_all | solution.py:268
  120.7 3.5 %all-to-all-start.4 = ((bf16[4,304,128]{2,1,0:T(8,128)(2,1)}), bf16[4,304,128]{2,1,0:T(8,128)(2,1)S(1)}, u32[]{:S(2)}, u32[]{:S(2)}) async-start(bf16[4,304,128]{2,1,0:T(8,128)(2,1)} %merge.1), calls=%async_computation.4 | async-start | bytes 622592 | tf_op jit(solution)/shard_map/all_to_all | solution.py:268
  124.1 2.3 %collective-permute-start.4 = (bf16[3,2,128,256]{3,2,1,0:T(8,128)(2,1)S(1)}, bf16[3,2,128,256]{3,2,1,0:T(8,128)(2,1)S(1)}, u32[]{:S(2)}, u32[]{:S(2)}) collective-permute-start(bf16[3,2,128,256]{3,2,1,0:T(8,128)(2,1)S(1)} %copy-done.6), channel_id=1, source_target_pairs={{0,32},{32,64},{64,96},{1,33},{33,65},{65,97},{2,34},{34,66},{66,9... | collective-permute-start | bytes 1179656 | tf_op jit(solution)/shard_map/ppermute | solution.py:260
  126.5 3.6 %collective-permute-start.5 = (bf16[3,2,128,256]{3,2,1,0:T(8,128)(2,1)S(1)}, bf16[3,2,128,256]{3,2,1,0:T(8,128)(2,1)S(1)}, u32[]{:S(2)}, u32[]{:S(2)}) collective-permute-start(bf16[3,2,128,256]{3,2,1,0:T(8,128)(2,1)S(1)} %copy-done.4), channel_id=1, source_target_pairs={{32,0},{64,32},{96,64},{33,1},{65,33},{97,65},{34,2},{66,34},{98,6... | collective-permute-start | bytes 1179656 | tf_op jit(solution)/shard_map/ppermute | solution.py:260
  130.0 5.2 %collective-permute-done.4.low_ref = bf16[3,2,128,256]{3,2,1,0:T(8,128)(2,1)S(1)} collective-permute-done((bf16[3,2,128,256]{3,2,1,0:T(8,128)(2,1)S(1)}, bf16[3,2,128,256]{3,2,1,0:T(8,128)(2,1)S(1)}, u32[]{:S(2)}, u32[]{:S(2)}) %collective-permute-start.4) | collective-permute-done | bytes 393248 | tf_op jit(solution)/shard_map/ppermute | solution.py:260
  135.2 1.9 %collective-permute-done.5.high_ref = bf16[3,2,128,256]{3,2,1,0:T(8,128)(2,1)S(1)} collective-permute-done((bf16[3,2,128,256]{3,2,1,0:T(8,128)(2,1)S(1)}, bf16[3,2,128,256]{3,2,1,0:T(8,128)(2,1)S(1)}, u32[]{:S(2)}, u32[]{:S(2)}) %collective-permute-start.5) | collective-permute-done | bytes 393248 | tf_op jit(solution)/shard_map/ppermute | solution.py:260
  137.2 5.8 %all-to-all-done.4.parts_ref = bf16[4,304,128]{2,1,0:T(8,128)(2,1)S(1)} async-done(((bf16[4,304,128]{2,1,0:T(8,128)(2,1)}), bf16[4,304,128]{2,1,0:T(8,128)(2,1)S(1)}, u32[]{:S(2)}, u32[]{:S(2)}) %all-to-all-start.4) | async-done | bytes 311328 | tf_op jit(solution)/shard_map/all_to_all | solution.py:268
  143.7 6.8 %all-to-all-start.5 = ((bf16[16,48,128]{2,1,0:T(8,128)(2,1)}), bf16[16,48,128]{2,1,0:T(8,128)(2,1)S(1)}, u32[]{:S(2)}, u32[]{:S(2)}) async-start(bf16[16,48,128]{2,1,0:T(8,128)(2,1)} %weight_total.1), calls=%async_computation.5 | async-start | bytes 393216 | tf_op jit(solution)/shard_map/all_to_all | solution.py:268
  150.6 3.4 %collective-permute-start.6 = (bf16[2,128,256]{2,1,0:T(8,128)(2,1)S(1)}, bf16[2,128,256]{2,1,0:T(8,128)(2,1)S(1)}, u32[]{:S(2)}, u32[]{:S(2)}) collective-permute-start(bf16[2,128,256]{2,1,0:T(8,128)(2,1)S(1)} %get-tuple-element.28), channel_id=1, source_target_pairs={{0,128},{128,256},{256,384},{1,129},{129,257},{257,385},{2,130},{1... | collective-permute-start | bytes 393224 | tf_op jit(solution)/shard_map/ppermute | solution.py:260
  154.0 1.3 collective-permute-start.7
  156.5 4.4 %collective-permute-done.7.high_ref = bf16[2,128,256]{2,1,0:T(8,128)(2,1)S(1)} collective-permute-done((bf16[2,128,256]{2,1,0:T(8,128)(2,1)S(1)}, bf16[2,128,256]{2,1,0:T(8,128)(2,1)S(1)}, u32[]{:S(2)}, u32[]{:S(2)}) %collective-permute-start.7) | collective-permute-done | bytes 131104 | tf_op jit(solution)/shard_map/ppermute | solution.py:260
  (40 shorter events, 14.3 us)
Async XLA Ops:
  1.5 15.2 %collective-permute-start.1 = (bf16[2,128,256]{2,1,0:T(8,128)(2,1)S(1)}, bf16[2,128,256]{2,1,0:T(8,128)(2,1)S(1)}, u32[]{:S(2)}, u32[]{:S(2)}) collective-permute-start(bf16[2,128,256]{2,1,0:T(8,128)(2,1)S(1)} %get-tuple-element.35), channel_id=1, source_target_pairs={{128,0},{256,128},{384,256},{129,1},{257,129},{385,257},{130,2},{2... | collective-permute-start | bytes 393224 | tf_op jit(solution)/shard_map/ppermute | solution.py:260
  2.8 13.9 %collective-permute-start = (bf16[2,128,256]{2,1,0:T(8,128)(2,1)S(1)}, bf16[2,128,256]{2,1,0:T(8,128)(2,1)S(1)}, u32[]{:S(2)}, u32[]{:S(2)}) collective-permute-start(bf16[2,128,256]{2,1,0:T(8,128)(2,1)S(1)} %get-tuple-element.35), channel_id=1, source_target_pairs={{0,128},{128,256},{256,384},{1,129},{129,257},{257,385},{2,130},{1... | collective-permute-start | bytes 393224 | tf_op jit(solution)/shard_map/ppermute | solution.py:260
  7.4 1.4 copy-start
  8.8 1.1 copy-start.1
  9.9 0.8 copy-start.2
  12.3 47.0 %copy-start.11 = (s32[2,6]{1,0:T(2,128)S(1)}, s32[2,6]{1,0:T(2,128)}, u32[]{:S(2)}) copy-start(s32[2,6]{1,0:T(2,128)} %win_ref.3) | copy-start | bytes 148
  12.3 51.6 %all-to-all-start = ((bf16[8,128,384]{2,1,0:T(8,128)(2,1)}), bf16[8,128,384]{2,1,0:T(8,128)(2,1)S(1)}, u32[]{:S(2)}, u32[]{:S(2)}) async-start(bf16[8,128,384]{2,1,0:T(8,128)(2,1)} %get-tuple-element.20), calls=%async_computation | async-start | bytes 1572864 | tf_op jit(solution)/shard_map/all_to_all | solution.py:268
  16.8 42.5 %collective-permute-start.3 = (bf16[3,2,128,256]{3,2,1,0:T(8,128)(2,1)S(1)}, bf16[3,2,128,256]{3,2,1,0:T(8,128)(2,1)S(1)}, u32[]{:S(2)}, u32[]{:S(2)}) collective-permute-start(bf16[3,2,128,256]{3,2,1,0:T(8,128)(2,1)S(1)} %pad_maximum_fusion.own_ref), channel_id=1, source_target_pairs={{32,0},{64,32},{96,64},{33,1},{65,33},{97,65},{34,2},{66,34},{98,6... | collective-permute-start | bytes 1179656 | tf_op jit(solution)/shard_map/ppermute | solution.py:260
  23.8 35.5 %collective-permute-start.2 = (bf16[3,2,128,256]{3,2,1,0:T(8,128)(2,1)S(1)}, bf16[3,2,128,256]{3,2,1,0:T(8,128)(2,1)S(1)}, u32[]{:S(2)}, u32[]{:S(2)}) collective-permute-start(bf16[3,2,128,256]{3,2,1,0:T(8,128)(2,1)S(1)} %pad_maximum_fusion.own_ref), channel_id=1, source_target_pairs={{0,32},{32,64},{64,96},{1,33},{33,65},{65,97},{2,34},{34,66},{66,9... | collective-permute-start | bytes 1179656 | tf_op jit(solution)/shard_map/ppermute | solution.py:260
  62.4 0.8 copy-start.7
  63.2 0.7 copy-start.9
  91.3 13.8 %all-to-all-start.2 = ((bf16[8,128,256]{2,1,0:T(8,128)(2,1)}), bf16[8,128,256]{2,1,0:T(8,128)(2,1)S(1)}, u32[]{:S(2)}, u32[]{:S(2)}) async-start(bf16[8,128,256]{2,1,0:T(8,128)(2,1)} %combine.1), calls=%async_computation.2 | async-start | bytes 1048576 | tf_op jit(solution)/shard_map/all_to_all | solution.py:268
  94.8 1.0 copy-start.8
  95.8 1.0 copy-start.10
  100.7 0.8 copy-start.3
  101.5 0.7 copy-start.5
  105.1 19.0 %copy-start.6 = (bf16[3,2,128,256]{3,2,1,0:T(8,128)(2,1)S(1)}, bf16[3,2,128,256]{3,2,1,0:T(8,128)(2,1)}, u32[]{:S(2)}) copy-start(bf16[3,2,128,256]{3,2,1,0:T(8,128)(2,1)} %copy-done.5) | copy-start | bytes 1179652
  105.1 21.4 %copy-start.4 = (bf16[3,2,128,256]{3,2,1,0:T(8,128)(2,1)S(1)}, bf16[3,2,128,256]{3,2,1,0:T(8,128)(2,1)}, u32[]{:S(2)}) copy-start(bf16[3,2,128,256]{3,2,1,0:T(8,128)(2,1)} %copy-done.3) | copy-start | bytes 1179652
  120.7 22.3 %all-to-all-start.4 = ((bf16[4,304,128]{2,1,0:T(8,128)(2,1)}), bf16[4,304,128]{2,1,0:T(8,128)(2,1)S(1)}, u32[]{:S(2)}, u32[]{:S(2)}) async-start(bf16[4,304,128]{2,1,0:T(8,128)(2,1)} %merge.1), calls=%async_computation.4 | async-start | bytes 622592 | tf_op jit(solution)/shard_map/all_to_all | solution.py:268
  124.1 11.1 %collective-permute-start.4 = (bf16[3,2,128,256]{3,2,1,0:T(8,128)(2,1)S(1)}, bf16[3,2,128,256]{3,2,1,0:T(8,128)(2,1)S(1)}, u32[]{:S(2)}, u32[]{:S(2)}) collective-permute-start(bf16[3,2,128,256]{3,2,1,0:T(8,128)(2,1)S(1)} %copy-done.6), channel_id=1, source_target_pairs={{0,32},{32,64},{64,96},{1,33},{33,65},{65,97},{2,34},{34,66},{66,9... | collective-permute-start | bytes 1179656 | tf_op jit(solution)/shard_map/ppermute | solution.py:260
  126.5 10.7 %collective-permute-start.5 = (bf16[3,2,128,256]{3,2,1,0:T(8,128)(2,1)S(1)}, bf16[3,2,128,256]{3,2,1,0:T(8,128)(2,1)S(1)}, u32[]{:S(2)}, u32[]{:S(2)}) collective-permute-start(bf16[3,2,128,256]{3,2,1,0:T(8,128)(2,1)S(1)} %copy-done.4), channel_id=1, source_target_pairs={{32,0},{64,32},{96,64},{33,1},{65,33},{97,65},{34,2},{66,34},{98,6... | collective-permute-start | bytes 1179656 | tf_op jit(solution)/shard_map/ppermute | solution.py:260
  143.7 18.5 %all-to-all-start.5 = ((bf16[16,48,128]{2,1,0:T(8,128)(2,1)}), bf16[16,48,128]{2,1,0:T(8,128)(2,1)S(1)}, u32[]{:S(2)}, u32[]{:S(2)}) async-start(bf16[16,48,128]{2,1,0:T(8,128)(2,1)} %weight_total.1), calls=%async_computation.5 | async-start | bytes 393216 | tf_op jit(solution)/shard_map/all_to_all | solution.py:268
  150.6 5.9 %collective-permute-start.6 = (bf16[2,128,256]{2,1,0:T(8,128)(2,1)S(1)}, bf16[2,128,256]{2,1,0:T(8,128)(2,1)S(1)}, u32[]{:S(2)}, u32[]{:S(2)}) collective-permute-start(bf16[2,128,256]{2,1,0:T(8,128)(2,1)S(1)} %get-tuple-element.28), channel_id=1, source_target_pairs={{0,128},{128,256},{256,384},{1,129},{129,257},{257,385},{2,130},{1... | collective-permute-start | bytes 393224 | tf_op jit(solution)/shard_map/ppermute | solution.py:260
  154.0 6.9 %collective-permute-start.7 = (bf16[2,128,256]{2,1,0:T(8,128)(2,1)S(1)}, bf16[2,128,256]{2,1,0:T(8,128)(2,1)S(1)}, u32[]{:S(2)}, u32[]{:S(2)}) collective-permute-start(bf16[2,128,256]{2,1,0:T(8,128)(2,1)S(1)} %get-tuple-element.29), channel_id=1, source_target_pairs={{128,0},{256,128},{384,256},{129,1},{257,129},{385,257},{130,2},{2... | collective-permute-start | bytes 393224 | tf_op jit(solution)/shard_map/ppermute | solution.py:260

commit v2 on v1

--- a/solution.py
+++ b/solution.py
@@ -21,6 +21,7 @@
 F32 = jnp.float32
 BF16 = jnp.bfloat16
 VM = pl.BlockSpec(memory_space=pltpu.VMEM)
+ANY = pl.BlockSpec(memory_space=pl.ANY)
 SMEM = pl.BlockSpec(memory_space=pltpu.SMEM)
 
 
@@ -36,11 +37,24 @@
     return slice(head * HD, (head + 1) * HD)
 
 
-def project_kernel(q_ref, g_ref, w_ref, out_ref, part_ref):
-    out_ref[0] = q_ref[...]
-    out_ref[1] = dot(g_ref[...], w_ref[...], 1, 1).astype(BF16)
-    for replica in range(REPLICAS):
-        part_ref[replica] = g_ref[:, replica * SLICE : (replica + 1) * SLICE]
+def project_kernel(q_ref, g_ref, w_ref, out_ref, mine_ref, theirs_ref, q_s, g_s, w_s, sems):
+    pairs = ((w_ref, w_s), (g_ref, g_s), (q_ref, q_s))
+    copies = [pltpu.make_async_copy(src, dst, sems.at[i]) for i, (src, dst) in enumerate(pairs)]
+    for copy in copies:
+        copy.start()
+    for copy in copies:
+        copy.wait()
+    grads = dot(g_s[...], w_s[...], 1, 1).astype(BF16)
+    for peer in range(SLABS):
+        out_ref[peer, 0] = q_s[...]
+        out_ref[peer, 1] = grads
+    place = lax.axis_index("x")
+    core = lax.axis_index("core")
+    for part_ref, side in ((mine_ref, core), (theirs_ref, 1 - core)):
+        for step in range(4):
+            replica = 2 * lax.rem(place + step, 4) + side
+            cols = pl.ds(pl.multiple_of(replica * SLICE, HD), SLICE)
+            part_ref[step] = g_s[:, cols]
 
 
 def row_bias(win_ref, head, dy):
@@ -194,15 +208,17 @@
         ref[...] = add3(own_ref[i], low_ref[i], high_ref[i])
 
 
-def frame_sum_kernel(own_ref, low_ref, high_ref, dk_ref, dv_ref):
-    for i, ref in enumerate((dk_ref, dv_ref)):
-        ref[...] = add3(own_ref[i], low_ref[i], high_ref[i])
-
-
-def weight_kernel(att_ref, grad_ref, out_ref):
-    att = att_ref[...].reshape(REPLICAS * TOK, WIDTH)
-    grad = grad_ref[...].reshape(REPLICAS * TOK, SLICE)
-    term = dot(att, grad, 0, 0).astype(BF16)
+def weight_kernel(att_ref, *refs):
+    grad_refs, out_ref = refs[:4], refs[4]
+    place = lax.axis_index("x")
+    core = lax.axis_index("core")
+    term = jnp.zeros((WIDTH, SLICE), F32)
+    for step, grad_ref in enumerate(grad_refs):
+        source = 2 * lax.rem(place + 4 - step, 4)
+        for other in range(2):
+            clip = source + (1 - core if other else core)
+            term = term + dot(att_ref[clip], grad_ref[other], 0, 0)
+    term = term.astype(BF16)
     for j in range(16):
         for c in range(3):
             piece = term[16 * j : 16 * (j + 1), HD * c : HD * (c + 1)]
@@ -223,22 +239,21 @@
         out_ref[peer, WIDTH:] = weight
 
 
-def weight_total_kernel(parts_ref, out_ref):
+def total_kernel(parts_ref, weight_ref, dq_ref):
     total = sum_over(parts_ref, SLABS, slice(WIDTH, WIDTH + 48))
     for i in range(16):
-        out_ref[i] = total
-
-
-def query_sum_kernel(parts_ref, dq_ref):
+        weight_ref[i] = total
     for head in range(HEADS):
         dq_ref[:, columns(head)] = sum_over(parts_ref, SLABS, columns(head))
 
 
-def unpack_kernel(parts_ref, out_ref):
+def finish_kernel(own_ref, low_ref, high_ref, parts_ref, dk_ref, dv_ref, weight_ref):
+    for i, ref in enumerate((dk_ref, dv_ref)):
+        ref[...] = add3(own_ref[i], low_ref[i], high_ref[i])
     for j in range(16):
         for c in range(3):
             piece = parts_ref[j, 16 * c : 16 * (c + 1), :].astype(F32)
-            out_ref[16 * j : 16 * (j + 1), HD * c : HD * (c + 1)] = piece
+            weight_ref[16 * j : 16 * (j + 1), HD * c : HD * (c + 1)] = piece
 
 
 def call(kernel, outs, specs, name, work=0, scratch=(), limit=4):
@@ -280,18 +295,29 @@
 
     kv = jnp.stack([keys.reshape(TOK, WIDTH), values.reshape(TOK, WIDTH)])
     kv_low, kv_high = neighbours(kv, kv, "tm")
+    asked, grad_mine, grad_theirs = call(
+        project_kernel,
+        (shape((SLABS, 2, TOK, WIDTH)), shape((4, TOK, SLICE)), shape((4, TOK, SLICE))),
+        [ANY] * 3,
+        "project",
+        2 * TOK * WIDTH * REPLICAS * SLICE,
+        [
+            pltpu.VMEM((TOK, WIDTH), BF16),
+            pltpu.VMEM((TOK, REPLICAS * SLICE), BF16),
+            pltpu.VMEM((WIDTH, REPLICAS * SLICE), BF16),
+            pltpu.SemaphoreType.DMA((3,)),
+        ],
+        60,
+    )(q, g, out_weight)
+    asked, kv_low, kv_high = lax.optimization_barrier((asked, kv_low, kv_high))
+    asked = exchange(asked, "zh")
     rows = jnp.stack([kv_low, kv, kv_high])
     rows_low, rows_high = neighbours(rows, rows, "y")
-    asked, grad_parts = call(
-        project_kernel,
-        (shape((2, TOK, WIDTH)), shape((REPLICAS, TOK, SLICE))),
-        3,
-        "project",
-        2 * TOK * WIDTH * REPLICAS * SLICE,
-        limit=8,
-    )(q, g, out_weight)
-    grad_slices = exchange(grad_parts, replica)
-    asked = lax.all_gather(asked, "zh")
+    grad_other = lax.ppermute(grad_theirs, "core", [(0, 1), (1, 0)])
+    grad_slices = [jnp.stack([grad_mine[step], grad_other[step]]) for step in range(4)]
+    for step in range(1, 4):
+        route = [(i, (i + step) % 4) for i in range(4)]
+        grad_slices[step] = lax.ppermute(grad_slices[step], "x", route)
     near = (rows_low, rows, rows_high)
 
     parts = call(
@@ -303,9 +329,9 @@
         [pltpu.VMEM((3, 3 * TOK, QUERIES), F32)],
         10,
     )(window, asked, *near)
-    parts = exchange(after(parts, grad_slices), "zh")
+    parts = exchange(after(parts, grad_slices[1]), "zh")
     att = call(combine_kernel, shape((REPLICAS, TOK, WIDTH)), 1, "combine")(parts)
-    att = exchange(att, replica)
+    att = exchange(after(att, *grad_slices[2:]), replica)
     grad_low, grad_own, grad_high, dq = call(
         backward_kernel,
         (row, row, row, shape((SLABS, WIDTH, HD))),
@@ -318,30 +344,26 @@
     weight = call(
         weight_kernel,
         shape((16, 48, HD)),
-        2,
+        5,
         "weight",
         2 * WIDTH * REPLICAS * TOK * SLICE,
-    )(after(att, grad_low), grad_slices)
+    )(after(att, grad_low), *grad_slices)
     weight = exchange(weight, tile)
     before, mid, behind = call(row_sum_kernel, (shape((2, TOK, WIDTH)),) * 3, 3, "row_sum", limit=8)(
         grad_own, from_low, from_high
     )
     from_before, from_behind = neighbours(before, behind, "tm")
-    dk, dv = call(frame_sum_kernel, (tokens, tokens), 3, "frame_sum")(
-        mid, from_before, from_behind
-    )
     merged = call(merge_kernel, shape((SLABS, WIDTH + 48, HD)), 2, "merge")(
         dq, weight
     )
     merged = exchange(merged, "zh")
-    weight = call(weight_total_kernel, shape((16, 48, HD)), 1, "weight_total")(
+    weight, dq = call(total_kernel, (shape((16, 48, HD)), tokens), 1, "total")(
         after(merged, from_low, from_high)
     )
     weight = exchange(weight, tile)
-    dq = call(query_sum_kernel, tokens, 1, "query_sum")(merged)
-    weight = call(unpack_kernel, shape((WIDTH, SLICE), F32), 1, "unpack")(
-        after(weight, dq, dk, dv)
-    )
+    dk, dv, weight = call(
+        finish_kernel, (tokens, tokens, shape((WIDTH, SLICE), F32)), 4, "finish"
+    )(mid, from_before, from_behind, weight)
     return dq.reshape(local), dk.reshape(local), dv.reshape(local), weight
 
 

time: 164 us -> 158 us (0.963)
  blocking collectives: 74.3 us -> 18.1 us
  starting transfers between devices: 43.5 us -> 73.4 us
  waiting for transfers between devices: 21.4 us -> 43.5 us
  local copies, waits for them, and re-layouts: 8.37 us -> 4.63 us
    all_gather x1 -> x0, blocking collectives: 33.5 us -> none  [on_device(): asked = lax.all_gather(asked, 'zh')]
    all_to_all x2 -> x1, blocking collectives: 40.7 us -> 18.1 us  [exchange(): return lax.all_to_all(block, axes, 0, 0, tiled=True)]
    all_to_all x4 -> x5, starting transfers between devices: 18.2 us -> 37.8 us  [exchange(): return lax.all_to_all(block, axes, 0, 0, tiled=True)]
    all_to_all x4 -> x5, waiting for transfers between devices: 8.69 us -> 24.9 us  [exchange(): return lax.all_to_all(block, axes, 0, 0, tiled=True)]
    ppermute x0 -> x4, starting transfers between devices: none -> 13.4 us  [the longest x3 11.4 us: on_device(): grad_slices[step] = lax.ppermute(grad_slices[step], 'x', route)]
    unnamed x24 -> x18, local copies, waits for them, and re-layouts: 8.37 us -> 3.5 us
    ppermute x4, starting transfers between devices: 13.2 us -> 8.51 us  [neighbours(): lax.ppermute(low_block, axis, down)]
    ppermute x4, waiting for transfers between devices: 6.31 us -> 10.4 us  [neighbours(): lax.ppermute(low_block, axis, down)]
  transfers between devices with their start and end apart: 12 -> 17, of which waited for: 6 -> 10; matrix products, arithmetic and copies ran while one was open for 0% -> 1% of each run, Pallas kernels for 6% -> 8%
where the time goes in v2:
time: 158 us; the launch traced here: 157 us
  starting transfers between devices  73.4 us (46%)
  waiting for transfers between devices  43.5 us (28%)
  blocking collectives  18.1 us (11%)
  Pallas kernels  14.9 us (9%)
  local copies, waits for them, and re-layouts  4.63 us (3%)
    all_to_all x5, starting transfers between devices, exchange(): return lax.all_to_all(block, axes, 0, 0, tiled=True)  37.8 us
    all_to_all x5, waiting for transfers between devices, exchange(): return lax.all_to_all(block, axes, 0, 0, tiled=True)  24.9 us
    all_to_all x1, blocking collectives, exchange(): return lax.all_to_all(block, axes, 0, 0, tiled=True)  18.1 us
    ppermute x4, starting transfers between devices, neighbours(): lax.ppermute(high_block, axis, up)  13.7 us
    ppermute x3, starting transfers between devices, on_device(): grad_slices[step] = lax.ppermute(grad_slices[step], 'x', route)  11.4 us
    ppermute x4, waiting for transfers between devices, neighbours(): lax.ppermute(low_block, axis, down)  10.4 us
    ppermute x4, starting transfers between devices, neighbours(): lax.ppermute(low_block, axis, down)  8.51 us
    ppermute x4, waiting for transfers between devices, neighbours(): lax.ppermute(high_block, axis, up)  8.22 us
  transfers between devices with their start and end apart: 17, of which 10 were waited for; matrix products, arithmetic and copies ran while one was open for 1% of the time, Pallas kernels for 8%

profile of v2, /device:TPU:8, one launch (start us, length us, event | category | flops | bytes accessed | tf_op | source)
XLA Modules:
  0.0 156.5 jit_solution(1204043844562344282)
XLA Ops:
  2.8 4.6 %collective-permute-start = (bf16[2,128,256]{2,1,0:T(8,128)(2,1)S(1)}, bf16[2,128,256]{2,1,0:T(8,128)(2,1)S(1)}, u32[]{:S(2)}, u32[]{:S(2)}) collective-permute-start(bf16[2,128,256]{2,1,0:T(8,128)(2,1)S(1)} %get-tuple-element.57), channel_id=1, source_target_pairs={{0,128},{128,256},{256,384},{1,129},{129,257},{257,385},{2,130},{1... | collective-permute-start | bytes 393224 | tf_op jit(solution)/shard_map/ppermute | solution.py:275
  7.4 3.2 %project.1 = (bf16[4,2,128,256]{3,2,1,0:T(8,128)(2,1)}, bf16[4,128,384]{2,1,0:T(8,128)(2,1)}, bf16[4,128,384]{2,1,0:T(8,128)(2,1)}) custom-call(bf16[128,256]{1,0:T(8,128)(2,1)} %bitcast.14, bf16[128,3072]{1,0:T(8,128)(2,1)} %bitcast.11, bf16[256,3072]{1,0:T(8,128)(2,1)} %w_ref.1), custom_call_target="tpu_custom_call" | custom-call | flops 201326592 | bytes 1048576 | tf_op jit(solution)/shard_map/project/pallas_call | solution.py:298
  10.6 15.1 %all-to-all-start = ((bf16[4,2,128,256]{3,2,1,0:T(8,128)(2,1)}), bf16[4,2,128,256]{3,2,1,0:T(8,128)(2,1)S(1)}, u32[]{:S(2)}, u32[]{:S(2)}) async-start(bf16[4,2,128,256]{3,2,1,0:T(8,128)(2,1)} %get-tuple-element.27), calls=%async_computation | async-start | bytes 1048576 | tf_op jit(solution)/shard_map/all_to_all | solution.py:283
  28.9 2.4 %collective-permute-start.3 = (bf16[3,2,128,256]{3,2,1,0:T(8,128)(2,1)S(1)}, bf16[3,2,128,256]{3,2,1,0:T(8,128)(2,1)S(1)}, u32[]{:S(2)}, u32[]{:S(2)}) collective-permute-start(bf16[3,2,128,256]{3,2,1,0:T(8,128)(2,1)S(1)} %pad_maximum_fusion.own_ref), channel_id=1, source_target_pairs={{32,0},{64,32},{96,64},{33,1},{65,33},{97,65},{34,2},{66,34},{98,6... | collective-permute-start | bytes 1179656 | tf_op jit(solution)/shard_map/ppermute | solution.py:275
  31.3 3.5 %collective-permute-start.2 = (bf16[3,2,128,256]{3,2,1,0:T(8,128)(2,1)S(1)}, bf16[3,2,128,256]{3,2,1,0:T(8,128)(2,1)S(1)}, u32[]{:S(2)}, u32[]{:S(2)}) collective-permute-start(bf16[3,2,128,256]{3,2,1,0:T(8,128)(2,1)S(1)} %pad_maximum_fusion.own_ref), channel_id=1, source_target_pairs={{0,32},{32,64},{64,96},{1,33},{33,65},{65,97},{2,34},{34,66},{66,9... | collective-permute-start | bytes 1179656 | tf_op jit(solution)/shard_map/ppermute | solution.py:275
  34.9 3.4 %collective-permute-start.5 = (bf16[2,128,384]{2,1,0:T(8,128)(2,1)S(1)}, bf16[2,128,384]{2,1,0:T(8,128)(2,1)S(1)}, u32[]{:S(2)}, u32[]{:S(2)}) collective-permute-start(bf16[2,128,384]{2,1,0:T(8,128)(2,1)S(1)} %pad_maximum_fusion.1), channel_id=1, source_target_pairs={{0,2},{2,4},{4,6},{6,0},{1,3},{3,5},{5,7},{7,1},{8,10},{10,12},{12... | collective-permute-start | bytes 589832 | tf_op jit(solution)/shard_map/ppermute | solution.py:320
  38.3 4.1 %collective-permute-done.3.high_ref = bf16[3,2,128,256]{3,2,1,0:T(8,128)(2,1)S(1)} collective-permute-done((bf16[3,2,128,256]{3,2,1,0:T(8,128)(2,1)S(1)}, bf16[3,2,128,256]{3,2,1,0:T(8,128)(2,1)S(1)}, u32[]{:S(2)}, u32[]{:S(2)}) %collective-permute-start.3) | collective-permute-done | bytes 393248 | tf_op jit(solution)/shard_map/ppermute | solution.py:275
  44.4 6.7 %all-to-all-done.asked_ref = bf16[4,2,128,256]{3,2,1,0:T(8,128)(2,1)S(1)} async-done(((bf16[4,2,128,256]{3,2,1,0:T(8,128)(2,1)}), bf16[4,2,128,256]{3,2,1,0:T(8,128)(2,1)S(1)}, u32[]{:S(2)}, u32[]{:S(2)}) %all-to-all-start) | async-done | bytes 524320 | tf_op jit(solution)/shard_map/all_to_all | solution.py:283
  51.1 3.8 %forward.1 = bf16[4,320,128]{2,1,0:T(8,128)(2,1)} custom-call(s32[2,6]{1,0:T(2,128)S(1)} %copy-done.8, bf16[4,2,128,256]{3,2,1,0:T(8,128)(2,1)S(1)} %all-to-all-done.asked_ref, bf16[3,2,128,256]{3,2,1,0:T(8,128)(2,1)S(1)} %collective-permute-done.2.low_ref, bf16[3,2,128,256]{3,2,1,0:T(8,128)(2,1)S(1)} %pad_maximum_fusion.own_ref, ...), custom_call_target="tpu_custom_call" | custom-call | flops 905969664 | bytes 1048576 | tf_op jit(solution)/shard_map/forward/pallas_call | solution.py:323
  54.9 9.5 %all-to-all-start.1 = ((bf16[4,320,128]{2,1,0:T(8,128)(2,1)}), bf16[4,320,128]{2,1,0:T(8,128)(2,1)S(1)}, u32[]{:S(2)}, u32[]{:S(2)}) async-start(bf16[4,320,128]{2,1,0:T(8,128)(2,1)} %forward.1), calls=%async_computation.1 | async-start | bytes 655360 | tf_op jit(solution)/shard_map/all_to_all | solution.py:283
  64.4 4.9 %collective-permute-start.6 = (bf16[2,128,384]{2,1,0:T(8,128)(2,1)S(1)}, bf16[2,128,384]{2,1,0:T(8,128)(2,1)S(1)}, u32[]{:S(2)}, u32[]{:S(2)}) collective-permute-start(bf16[2,128,384]{2,1,0:T(8,128)(2,1)S(1)} %pad_maximum_fusion.2), channel_id=1, source_target_pairs={{0,4},{2,6},{4,0},{6,2},{1,5},{3,7},{5,1},{7,3},{8,12},{10,14},{12... | collective-permute-start | bytes 589832 | tf_op jit(solution)/shard_map/ppermute | solution.py:320
  69.4 3.1 %collective-permute-start.7 = (bf16[2,128,384]{2,1,0:T(8,128)(2,1)S(1)}, bf16[2,128,384]{2,1,0:T(8,128)(2,1)S(1)}, u32[]{:S(2)}, u32[]{:S(2)}) collective-permute-start(bf16[2,128,384]{2,1,0:T(8,128)(2,1)S(1)} %pad_maximum_fusion.3), channel_id=1, source_target_pairs={{0,6},{2,0},{4,2},{6,4},{1,7},{3,1},{5,3},{7,5},{8,14},{10,8},{12,... | collective-permute-start | bytes 589832 | tf_op jit(solution)/shard_map/ppermute | solution.py:320
  72.5 8.1 %all-to-all-done.1.parts_ref = bf16[4,320,128]{2,1,0:T(8,128)(2,1)S(1)} async-done(((bf16[4,320,128]{2,1,0:T(8,128)(2,1)}), bf16[4,320,128]{2,1,0:T(8,128)(2,1)S(1)}, u32[]{:S(2)}, u32[]{:S(2)}) %all-to-all-start.1) | async-done | bytes 327712 | tf_op jit(solution)/shard_map/all_to_all | solution.py:283
  81.5 4.4 %all-to-all-start.2 = ((bf16[8,128,256]{2,1,0:T(8,128)(2,1)}), bf16[8,128,256]{2,1,0:T(8,128)(2,1)S(1)}, u32[]{:S(2)}, u32[]{:S(2)}) async-start(bf16[8,128,256]{2,1,0:T(8,128)(2,1)} %combine.1), calls=%async_computation.2 | async-start | bytes 1048576 | tf_op jit(solution)/shard_map/all_to_all | solution.py:283
  88.0 3.9 %backward.1 = (bf16[3,2,128,256]{3,2,1,0:T(8,128)(2,1)S(1)}, bf16[3,2,128,256]{3,2,1,0:T(8,128)(2,1)S(1)}, bf16[3,2,128,256]{3,2,1,0:T(8,128)(2,1)S(1)}, bf16[4,256,128]{2,1,0:T(8,128)(2,1)S(1)}) custom-call(s32[2,6]{1,0:T(2,128)S(1)} %copy-done.8, bf16[4,2,128,256]{3,2,1,0:T(8,128)(2,1)S(1)} %all-to-all-done.asked_ref, ...), custom_call_target="tpu_custom_call" | custom-call | flops 1509949440 | bytes 1048576 | tf_op jit(solution)/shard_map/backward/pallas_call | solution.py:335
  93.4 2.9 %all-to-all-done.2.att_ref = bf16[8,128,256]{2,1,0:T(8,128)(2,1)S(1)} async-done(((bf16[8,128,256]{2,1,0:T(8,128)(2,1)}), bf16[8,128,256]{2,1,0:T(8,128)(2,1)S(1)}, u32[]{:S(2)}, u32[]{:S(2)}) %all-to-all-start.2) | async-done | bytes 524320 | tf_op jit(solution)/shard_map/all_to_all | solution.py:283
  96.9 18.1 %all_to_all.30.weight_ref = bf16[16,48,128]{2,1,0:T(8,128)(2,1)S(1)} all-to-all(bf16[16,48,128]{2,1,0:T(8,128)(2,1)S(1)} %weight.1), channel_id=1, replica_groups=mesh['tm'=4,'y'=4,'zh'=4,'x'=4,'core'=2] {'tm','y'}, dimensions={0} | all-to-all | bytes 393216 | tf_op jit(solution)/shard_map/all_to_all | solution.py:283
  115.8 4.1 %all-to-all-start.4 = ((bf16[4,304,128]{2,1,0:T(8,128)(2,1)}), bf16[4,304,128]{2,1,0:T(8,128)(2,1)S(1)}, u32[]{:S(2)}, u32[]{:S(2)}) async-start(bf16[4,304,128]{2,1,0:T(8,128)(2,1)} %merge.1), calls=%async_computation.4 | async-start | bytes 622592 | tf_op jit(solution)/shard_map/all_to_all | solution.py:283
  122.2 3.6 %collective-permute-start.9 = (bf16[3,2,128,256]{3,2,1,0:T(8,128)(2,1)S(1)}, bf16[3,2,128,256]{3,2,1,0:T(8,128)(2,1)S(1)}, u32[]{:S(2)}, u32[]{:S(2)}) collective-permute-start(bf16[3,2,128,256]{3,2,1,0:T(8,128)(2,1)S(1)} %copy-done.5), channel_id=1, source_target_pairs={{32,0},{64,32},{96,64},{33,1},{65,33},{97,65},{34,2},{66,34},{98,6... | collective-permute-start | bytes 1179656 | tf_op jit(solution)/shard_map/ppermute | solution.py:275
  125.8 4.9 %collective-permute-done.8.low_ref = bf16[3,2,128,256]{3,2,1,0:T(8,128)(2,1)S(1)} collective-permute-done((bf16[3,2,128,256]{3,2,1,0:T(8,128)(2,1)S(1)}, bf16[3,2,128,256]{3,2,1,0:T(8,128)(2,1)S(1)}, u32[]{:S(2)}, u32[]{:S(2)}) %collective-permute-start.8) | collective-permute-done | bytes 393248 | tf_op jit(solution)/shard_map/ppermute | solution.py:275
  132.7 7.2 %all-to-all-done.4.parts_ref = bf16[4,304,128]{2,1,0:T(8,128)(2,1)S(1)} async-done(((bf16[4,304,128]{2,1,0:T(8,128)(2,1)}), bf16[4,304,128]{2,1,0:T(8,128)(2,1)S(1)}, u32[]{:S(2)}, u32[]{:S(2)}) %all-to-all-start.4) | async-done | bytes 311328 | tf_op jit(solution)/shard_map/all_to_all | solution.py:283
  140.6 4.7 %all-to-all-start.5 = ((bf16[16,48,128]{2,1,0:T(8,128)(2,1)}), bf16[16,48,128]{2,1,0:T(8,128)(2,1)S(1)}, u32[]{:S(2)}, u32[]{:S(2)}) async-start(bf16[16,48,128]{2,1,0:T(8,128)(2,1)} %get-tuple-element.44), calls=%async_computation.5 | async-start | bytes 393216 | tf_op jit(solution)/shard_map/all_to_all | solution.py:283
  145.5 3.4 %collective-permute-start.10 = (bf16[2,128,256]{2,1,0:T(8,128)(2,1)S(1)}, bf16[2,128,256]{2,1,0:T(8,128)(2,1)S(1)}, u32[]{:S(2)}, u32[]{:S(2)}) collective-permute-start(bf16[2,128,256]{2,1,0:T(8,128)(2,1)S(1)} %get-tuple-element.42), channel_id=1, source_target_pairs={{0,128},{128,256},{256,384},{1,129},{129,257},{257,385},{2,130},{1... | collective-permute-start | bytes 393224 | tf_op jit(solution)/shard_map/ppermute | solution.py:275
  151.3 4.4 %collective-permute-done.11.high_ref = bf16[2,128,256]{2,1,0:T(8,128)(2,1)S(1)} collective-permute-done((bf16[2,128,256]{2,1,0:T(8,128)(2,1)S(1)}, bf16[2,128,256]{2,1,0:T(8,128)(2,1)S(1)}, u32[]{:S(2)}, u32[]{:S(2)}) %collective-permute-start.11) | collective-permute-done | bytes 131104 | tf_op jit(solution)/shard_map/ppermute | solution.py:275
  (46 shorter events, 21.8 us)
Async XLA Ops:
  1.5 9.1 %collective-permute-start.1 = (bf16[2,128,256]{2,1,0:T(8,128)(2,1)S(1)}, bf16[2,128,256]{2,1,0:T(8,128)(2,1)S(1)}, u32[]{:S(2)}, u32[]{:S(2)}) collective-permute-start(bf16[2,128,256]{2,1,0:T(8,128)(2,1)S(1)} %get-tuple-element.57), channel_id=1, source_target_pairs={{128,0},{256,128},{384,256},{129,1},{257,129},{385,257},{130,2},{2... | collective-permute-start | bytes 393224 | tf_op jit(solution)/shard_map/ppermute | solution.py:275
  2.8 7.8 %collective-permute-start = (bf16[2,128,256]{2,1,0:T(8,128)(2,1)S(1)}, bf16[2,128,256]{2,1,0:T(8,128)(2,1)S(1)}, u32[]{:S(2)}, u32[]{:S(2)}) collective-permute-start(bf16[2,128,256]{2,1,0:T(8,128)(2,1)S(1)} %get-tuple-element.57), channel_id=1, source_target_pairs={{0,128},{128,256},{256,384},{1,129},{129,257},{257,385},{2,130},{1... | collective-permute-start | bytes 393224 | tf_op jit(solution)/shard_map/ppermute | solution.py:275
  10.6 40.5 %all-to-all-start = ((bf16[4,2,128,256]{3,2,1,0:T(8,128)(2,1)}), bf16[4,2,128,256]{3,2,1,0:T(8,128)(2,1)S(1)}, u32[]{:S(2)}, u32[]{:S(2)}) async-start(bf16[4,2,128,256]{3,2,1,0:T(8,128)(2,1)} %get-tuple-element.27), calls=%async_computation | async-start | bytes 1048576 | tf_op jit(solution)/shard_map/all_to_all | solution.py:283
  25.7 25.4 %copy-start.8 = (s32[2,6]{1,0:T(2,128)S(1)}, s32[2,6]{1,0:T(2,128)}, u32[]{:S(2)}) copy-start(s32[2,6]{1,0:T(2,128)} %win_ref.3) | copy-start | bytes 148
  25.7 9.0 %collective-permute-start.4 = (bf16[4,128,384]{2,1,0:T(8,128)(2,1)}, bf16[4,128,384]{2,1,0:T(8,128)(2,1)S(1)}, u32[]{:S(2)}, u32[]{:S(2)}) collective-permute-start(bf16[4,128,384]{2,1,0:T(8,128)(2,1)} %get-tuple-element.31), channel_id=1, source_target_pairs={{0,1},{1,0},{2,3},{3,2},{4,5},{5,4},{6,7},{7,6},{8,9},{9,8},{10,11... | collective-permute-start | bytes 1179656 | tf_op jit(solution)/shard_map/ppermute | solution.py:316
  28.9 13.4 %collective-permute-start.3 = (bf16[3,2,128,256]{3,2,1,0:T(8,128)(2,1)S(1)}, bf16[3,2,128,256]{3,2,1,0:T(8,128)(2,1)S(1)}, u32[]{:S(2)}, u32[]{:S(2)}) collective-permute-start(bf16[3,2,128,256]{3,2,1,0:T(8,128)(2,1)S(1)} %pad_maximum_fusion.own_ref), channel_id=1, source_target_pairs={{32,0},{64,32},{96,64},{33,1},{65,33},{97,65},{34,2},{66,34},{98,6... | collective-permute-start | bytes 1179656 | tf_op jit(solution)/shard_map/ppermute | solution.py:275
  31.3 13.1 %collective-permute-start.2 = (bf16[3,2,128,256]{3,2,1,0:T(8,128)(2,1)S(1)}, bf16[3,2,128,256]{3,2,1,0:T(8,128)(2,1)S(1)}, u32[]{:S(2)}, u32[]{:S(2)}) collective-permute-start(bf16[3,2,128,256]{3,2,1,0:T(8,128)(2,1)S(1)} %pad_maximum_fusion.own_ref), channel_id=1, source_target_pairs={{0,32},{32,64},{64,96},{1,33},{33,65},{65,97},{2,34},{34,66},{66,9... | collective-permute-start | bytes 1179656 | tf_op jit(solution)/shard_map/ppermute | solution.py:275
  34.9 20.1 %collective-permute-start.5 = (bf16[2,128,384]{2,1,0:T(8,128)(2,1)S(1)}, bf16[2,128,384]{2,1,0:T(8,128)(2,1)S(1)}, u32[]{:S(2)}, u32[]{:S(2)}) collective-permute-start(bf16[2,128,384]{2,1,0:T(8,128)(2,1)S(1)} %pad_maximum_fusion.1), channel_id=1, source_target_pairs={{0,2},{2,4},{4,6},{6,0},{1,3},{3,5},{5,7},{7,1},{8,10},{10,12},{12... | collective-permute-start | bytes 589832 | tf_op jit(solution)/shard_map/ppermute | solution.py:320
  42.3 12.6 %copy-start = (bf16[3,2,128,256]{3,2,1,0:T(8,128)(2,1)}, bf16[3,2,128,256]{3,2,1,0:T(8,128)(2,1)S(1)}, u32[]{:S(2)}) copy-start(bf16[3,2,128,256]{3,2,1,0:T(8,128)(2,1)S(1)} %collective-permute-done.3.high_ref) | copy-start | bytes 1179652
  44.4 10.5 %copy-start.2 = (bf16[3,2,128,256]{3,2,1,0:T(8,128)(2,1)}, bf16[3,2,128,256]{3,2,1,0:T(8,128)(2,1)S(1)}, u32[]{:S(2)}) copy-start(bf16[3,2,128,256]{3,2,1,0:T(8,128)(2,1)S(1)} %collective-permute-done.2.low_ref) | copy-start | bytes 1179652
  54.9 25.6 %all-to-all-start.1 = ((bf16[4,320,128]{2,1,0:T(8,128)(2,1)}), bf16[4,320,128]{2,1,0:T(8,128)(2,1)S(1)}, u32[]{:S(2)}, u32[]{:S(2)}) async-start(bf16[4,320,128]{2,1,0:T(8,128)(2,1)} %forward.1), calls=%async_computation.1 | async-start | bytes 655360 | tf_op jit(solution)/shard_map/all_to_all | solution.py:283
  64.4 17.1 %collective-permute-start.6 = (bf16[2,128,384]{2,1,0:T(8,128)(2,1)S(1)}, bf16[2,128,384]{2,1,0:T(8,128)(2,1)S(1)}, u32[]{:S(2)}, u32[]{:S(2)}) collective-permute-start(bf16[2,128,384]{2,1,0:T(8,128)(2,1)S(1)} %pad_maximum_fusion.2), channel_id=1, source_target_pairs={{0,4},{2,6},{4,0},{6,2},{1,5},{3,7},{5,1},{7,3},{8,12},{10,14},{12... | collective-permute-start | bytes 589832 | tf_op jit(solution)/shard_map/ppermute | solution.py:320
  69.4 12.2 %collective-permute-start.7 = (bf16[2,128,384]{2,1,0:T(8,128)(2,1)S(1)}, bf16[2,128,384]{2,1,0:T(8,128)(2,1)S(1)}, u32[]{:S(2)}, u32[]{:S(2)}) collective-permute-start(bf16[2,128,384]{2,1,0:T(8,128)(2,1)S(1)} %pad_maximum_fusion.3), channel_id=1, source_target_pairs={{0,6},{2,0},{4,2},{6,4},{1,7},{3,1},{5,3},{7,5},{8,14},{10,8},{12,... | collective-permute-start | bytes 589832 | tf_op jit(solution)/shard_map/ppermute | solution.py:320
  81.5 14.8 %all-to-all-start.2 = ((bf16[8,128,256]{2,1,0:T(8,128)(2,1)}), bf16[8,128,256]{2,1,0:T(8,128)(2,1)S(1)}, u32[]{:S(2)}, u32[]{:S(2)}) async-start(bf16[8,128,256]{2,1,0:T(8,128)(2,1)} %combine.1), calls=%async_computation.2 | async-start | bytes 1048576 | tf_op jit(solution)/shard_map/all_to_all | solution.py:283
  86.0 1.0 copy-start.1
  87.0 1.0 copy-start.3
  96.3 23.6 %copy-start.7 = (bf16[3,2,128,256]{3,2,1,0:T(8,128)(2,1)S(1)}, bf16[3,2,128,256]{3,2,1,0:T(8,128)(2,1)}, u32[]{:S(2)}) copy-start(bf16[3,2,128,256]{3,2,1,0:T(8,128)(2,1)} %copy-done.6) | copy-start | bytes 1179652
  96.3 25.9 %copy-start.5 = (bf16[3,2,128,256]{3,2,1,0:T(8,128)(2,1)S(1)}, bf16[3,2,128,256]{3,2,1,0:T(8,128)(2,1)}, u32[]{:S(2)}) copy-start(bf16[3,2,128,256]{3,2,1,0:T(8,128)(2,1)} %copy-done.4) | copy-start | bytes 1179652
  115.8 24.0 %all-to-all-start.4 = ((bf16[4,304,128]{2,1,0:T(8,128)(2,1)}), bf16[4,304,128]{2,1,0:T(8,128)(2,1)S(1)}, u32[]{:S(2)}, u32[]{:S(2)}) async-start(bf16[4,304,128]{2,1,0:T(8,128)(2,1)} %merge.1), calls=%async_computation.4 | async-start | bytes 622592 | tf_op jit(solution)/shard_map/all_to_all | solution.py:283
  119.9 10.8 %collective-permute-start.8 = (bf16[3,2,128,256]{3,2,1,0:T(8,128)(2,1)S(1)}, bf16[3,2,128,256]{3,2,1,0:T(8,128)(2,1)S(1)}, u32[]{:S(2)}, u32[]{:S(2)}) collective-permute-start(bf16[3,2,128,256]{3,2,1,0:T(8,128)(2,1)S(1)} %copy-done.7), channel_id=1, source_target_pairs={{0,32},{32,64},{64,96},{1,33},{33,65},{65,97},{2,34},{34,66},{66,9... | collective-permute-start | bytes 1179656 | tf_op jit(solution)/shard_map/ppermute | solution.py:275
  122.2 10.5 %collective-permute-start.9 = (bf16[3,2,128,256]{3,2,1,0:T(8,128)(2,1)S(1)}, bf16[3,2,128,256]{3,2,1,0:T(8,128)(2,1)S(1)}, u32[]{:S(2)}, u32[]{:S(2)}) collective-permute-start(bf16[3,2,128,256]{3,2,1,0:T(8,128)(2,1)S(1)} %copy-done.5), channel_id=1, source_target_pairs={{32,0},{64,32},{96,64},{33,1},{65,33},{97,65},{34,2},{66,34},{98,6... | collective-permute-start | bytes 1179656 | tf_op jit(solution)/shard_map/ppermute | solution.py:275
  140.6 15.1 %all-to-all-start.5 = ((bf16[16,48,128]{2,1,0:T(8,128)(2,1)}), bf16[16,48,128]{2,1,0:T(8,128)(2,1)S(1)}, u32[]{:S(2)}, u32[]{:S(2)}) async-start(bf16[16,48,128]{2,1,0:T(8,128)(2,1)} %get-tuple-element.44), calls=%async_computation.5 | async-start | bytes 393216 | tf_op jit(solution)/shard_map/all_to_all | solution.py:283
  145.5 5.9 %collective-permute-start.10 = (bf16[2,128,256]{2,1,0:T(8,128)(2,1)S(1)}, bf16[2,128,256]{2,1,0:T(8,128)(2,1)S(1)}, u32[]{:S(2)}, u32[]{:S(2)}) collective-permute-start(bf16[2,128,256]{2,1,0:T(8,128)(2,1)S(1)} %get-tuple-element.42), channel_id=1, source_target_pairs={{0,128},{128,256},{256,384},{1,129},{129,257},{257,385},{2,130},{1... | collective-permute-start | bytes 393224 | tf_op jit(solution)/shard_map/ppermute | solution.py:275
  148.9 6.9 %collective-permute-start.11 = (bf16[2,128,256]{2,1,0:T(8,128)(2,1)S(1)}, bf16[2,128,256]{2,1,0:T(8,128)(2,1)S(1)}, u32[]{:S(2)}, u32[]{:S(2)}) collective-permute-start(bf16[2,128,256]{2,1,0:T(8,128)(2,1)S(1)} %get-tuple-element.43), channel_id=1, source_target_pairs={{128,0},{256,128},{384,256},{129,1},{257,129},{385,257},{130,2},{2... | collective-permute-start | bytes 393224 | tf_op jit(solution)/shard_map/ppermute | solution.py:275
  (2 other events, 1.5 us)

commit v3 on v2

--- a/solution.py
+++ b/solution.py
@@ -338,7 +338,7 @@
         [SMEM] + [VM] * 5,
         "backward",
         5 * pair_work,
-        limit=10,
+        limit=60,
     )(window, asked, parts, *near)
     from_low, from_high = neighbours(grad_low, grad_high, "y")
     weight = call(

time: 158 us -> 158 us (level)
  local copies, waits for them, and re-layouts: 4.63 us -> 1.16 us
  Pallas kernels: 14.9 us -> 16.7 us
  waiting for transfers between devices: 43.5 us -> 45.1 us
    unnamed x18 -> x20, local copies, waits for them, and re-layouts: 3.5 us -> 0.04 us
    pallas_call x1, Pallas kernels: 3.89 us -> 5.61 us  [on_device(): call(backward_kernel, (row, row, row, shape((SLABS, WIDTH, HD))), [SMEM]...]
    all_to_all x5, waiting for transfers between devices: 24.9 us -> 26.5 us  [exchange(): return lax.all_to_all(block, axes, 0, 0, tiled=True)]
  transfers between devices with their start and end apart: 17 -> 17, of which waited for: 10 -> 10; matrix products, arithmetic and copies ran while one was open for 1% -> 1% of each run, Pallas kernels for 8% -> 9%
where the time goes in v3:
time: 158 us; the launch traced here: 157 us
  starting transfers between devices  73.4 us (46%)
  waiting for transfers between devices  45.1 us (29%)
  blocking collectives  18.4 us (12%)
  Pallas kernels  16.7 us (11%)
    all_to_all x5, starting transfers between devices, exchange(): return lax.all_to_all(block, axes, 0, 0, tiled=True)  37.8 us
    all_to_all x5, waiting for transfers between devices, exchange(): return lax.all_to_all(block, axes, 0, 0, tiled=True)  26.5 us
    all_to_all x1, blocking collectives, exchange(): return lax.all_to_all(block, axes, 0, 0, tiled=True)  18.4 us
    ppermute x4, starting transfers between devices, neighbours(): lax.ppermute(high_block, axis, up)  13.7 us
    ppermute x3, starting transfers between devices, on_device(): grad_slices[step] = lax.ppermute(grad_slices[step], 'x', route)  11.4 us
    ppermute x4, waiting for transfers between devices, neighbours(): lax.ppermute(low_block, axis, down)  10.4 us
    ppermute x4, starting transfers between devices, neighbours(): lax.ppermute(low_block, axis, down)  8.5 us
    ppermute x4, waiting for transfers between devices, neighbours(): lax.ppermute(high_block, axis, up)  8.23 us
  transfers between devices with their start and end apart: 17, of which 10 were waited for; matrix products, arithmetic and copies ran while one was open for 1% of the time, Pallas kernels for 9%

profile of v3, /device:TPU:8, one launch (start us, length us, event | category | flops | bytes accessed | tf_op | source)
XLA Modules:
  0.0 156.8 jit_solution(6853462246293176412)
XLA Ops:
  2.8 4.6 %collective-permute-start = (bf16[2,128,256]{2,1,0:T(8,128)(2,1)S(1)}, bf16[2,128,256]{2,1,0:T(8,128)(2,1)S(1)}, u32[]{:S(2)}, u32[]{:S(2)}) collective-permute-start(bf16[2,128,256]{2,1,0:T(8,128)(2,1)S(1)} %get-tuple-element.57), channel_id=1, source_target_pairs={{0,128},{128,256},{256,384},{1,129},{129,257},{257,385},{2,130},{1... | collective-permute-start | bytes 393224 | tf_op jit(solution)/shard_map/ppermute | solution.py:275
  7.4 3.2 %project.1 = (bf16[4,2,128,256]{3,2,1,0:T(8,128)(2,1)}, bf16[4,128,384]{2,1,0:T(8,128)(2,1)}, bf16[4,128,384]{2,1,0:T(8,128)(2,1)}) custom-call(bf16[128,256]{1,0:T(8,128)(2,1)} %bitcast.14, bf16[128,3072]{1,0:T(8,128)(2,1)} %bitcast.11, bf16[256,3072]{1,0:T(8,128)(2,1)} %w_ref.1), custom_call_target="tpu_custom_call" | custom-call | flops 201326592 | bytes 1048576 | tf_op jit(solution)/shard_map/project/pallas_call | solution.py:298
  10.6 15.1 %all-to-all-start = ((bf16[4,2,128,256]{3,2,1,0:T(8,128)(2,1)}), bf16[4,2,128,256]{3,2,1,0:T(8,128)(2,1)S(1)}, u32[]{:S(2)}, u32[]{:S(2)}) async-start(bf16[4,2,128,256]{3,2,1,0:T(8,128)(2,1)} %get-tuple-element.27), calls=%async_computation | async-start | bytes 1048576 | tf_op jit(solution)/shard_map/all_to_all | solution.py:283
  28.9 2.4 %collective-permute-start.3 = (bf16[3,2,128,256]{3,2,1,0:T(8,128)(2,1)S(1)}, bf16[3,2,128,256]{3,2,1,0:T(8,128)(2,1)S(1)}, u32[]{:S(2)}, u32[]{:S(2)}) collective-permute-start(bf16[3,2,128,256]{3,2,1,0:T(8,128)(2,1)S(1)} %pad_maximum_fusion.own_ref), channel_id=1, source_target_pairs={{32,0},{64,32},{96,64},{33,1},{65,33},{97,65},{34,2},{66,34},{98,6... | collective-permute-start | bytes 1179656 | tf_op jit(solution)/shard_map/ppermute | solution.py:275
  31.3 3.5 %collective-permute-start.2 = (bf16[3,2,128,256]{3,2,1,0:T(8,128)(2,1)S(1)}, bf16[3,2,128,256]{3,2,1,0:T(8,128)(2,1)S(1)}, u32[]{:S(2)}, u32[]{:S(2)}) collective-permute-start(bf16[3,2,128,256]{3,2,1,0:T(8,128)(2,1)S(1)} %pad_maximum_fusion.own_ref), channel_id=1, source_target_pairs={{0,32},{32,64},{64,96},{1,33},{33,65},{65,97},{2,34},{34,66},{66,9... | collective-permute-start | bytes 1179656 | tf_op jit(solution)/shard_map/ppermute | solution.py:275
  34.9 3.4 %collective-permute-start.5 = (bf16[2,128,384]{2,1,0:T(8,128)(2,1)S(1)}, bf16[2,128,384]{2,1,0:T(8,128)(2,1)S(1)}, u32[]{:S(2)}, u32[]{:S(2)}) collective-permute-start(bf16[2,128,384]{2,1,0:T(8,128)(2,1)S(1)} %pad_maximum_fusion.1), channel_id=1, source_target_pairs={{0,2},{2,4},{4,6},{6,0},{1,3},{3,5},{5,7},{7,1},{8,10},{10,12},{12... | collective-permute-start | bytes 589832 | tf_op jit(solution)/shard_map/ppermute | solution.py:320
  38.3 4.1 %collective-permute-done.3.high_ref = bf16[3,2,128,256]{3,2,1,0:T(8,128)(2,1)S(1)} collective-permute-done((bf16[3,2,128,256]{3,2,1,0:T(8,128)(2,1)S(1)}, bf16[3,2,128,256]{3,2,1,0:T(8,128)(2,1)S(1)}, u32[]{:S(2)}, u32[]{:S(2)}) %collective-permute-start.3) | collective-permute-done | bytes 393248 | tf_op jit(solution)/shard_map/ppermute | solution.py:275
  44.4 6.7 %all-to-all-done.asked_ref = bf16[4,2,128,256]{3,2,1,0:T(8,128)(2,1)S(1)} async-done(((bf16[4,2,128,256]{3,2,1,0:T(8,128)(2,1)}), bf16[4,2,128,256]{3,2,1,0:T(8,128)(2,1)S(1)}, u32[]{:S(2)}, u32[]{:S(2)}) %all-to-all-start) | async-done | bytes 524320 | tf_op jit(solution)/shard_map/all_to_all | solution.py:283
  51.1 3.9 %forward.1 = bf16[4,320,128]{2,1,0:T(8,128)(2,1)} custom-call(s32[2,6]{1,0:T(2,128)S(1)} %copy-done.7, bf16[4,2,128,256]{3,2,1,0:T(8,128)(2,1)S(1)} %all-to-all-done.asked_ref, bf16[3,2,128,256]{3,2,1,0:T(8,128)(2,1)S(1)} %collective-permute-done.2.low_ref, bf16[3,2,128,256]{3,2,1,0:T(8,128)(2,1)S(1)} %pad_maximum_fusion.own_ref, ...), custom_call_target="tpu_custom_call" | custom-call | flops 905969664 | bytes 1048576 | tf_op jit(solution)/shard_map/forward/pallas_call | solution.py:323
  55.0 9.5 %all-to-all-start.1 = ((bf16[4,320,128]{2,1,0:T(8,128)(2,1)}), bf16[4,320,128]{2,1,0:T(8,128)(2,1)S(1)}, u32[]{:S(2)}, u32[]{:S(2)}) async-start(bf16[4,320,128]{2,1,0:T(8,128)(2,1)} %forward.1), calls=%async_computation.1 | async-start | bytes 655360 | tf_op jit(solution)/shard_map/all_to_all | solution.py:283
  64.5 4.9 %collective-permute-start.6 = (bf16[2,128,384]{2,1,0:T(8,128)(2,1)S(1)}, bf16[2,128,384]{2,1,0:T(8,128)(2,1)S(1)}, u32[]{:S(2)}, u32[]{:S(2)}) collective-permute-start(bf16[2,128,384]{2,1,0:T(8,128)(2,1)S(1)} %pad_maximum_fusion.2), channel_id=1, source_target_pairs={{0,4},{2,6},{4,0},{6,2},{1,5},{3,7},{5,1},{7,3},{8,12},{10,14},{12... | collective-permute-start | bytes 589832 | tf_op jit(solution)/shard_map/ppermute | solution.py:320
  69.5 3.1 %collective-permute-start.7 = (bf16[2,128,384]{2,1,0:T(8,128)(2,1)S(1)}, bf16[2,128,384]{2,1,0:T(8,128)(2,1)S(1)}, u32[]{:S(2)}, u32[]{:S(2)}) collective-permute-start(bf16[2,128,384]{2,1,0:T(8,128)(2,1)S(1)} %pad_maximum_fusion.3), channel_id=1, source_target_pairs={{0,6},{2,0},{4,2},{6,4},{1,7},{3,1},{5,3},{7,5},{8,14},{10,8},{12,... | collective-permute-start | bytes 589832 | tf_op jit(solution)/shard_map/ppermute | solution.py:320
  72.5 8.2 %all-to-all-done.1.parts_ref = bf16[4,320,128]{2,1,0:T(8,128)(2,1)S(1)} async-done(((bf16[4,320,128]{2,1,0:T(8,128)(2,1)}), bf16[4,320,128]{2,1,0:T(8,128)(2,1)S(1)}, u32[]{:S(2)}, u32[]{:S(2)}) %all-to-all-start.1) | async-done | bytes 327712 | tf_op jit(solution)/shard_map/all_to_all | solution.py:283
  81.8 4.1 %all-to-all-start.2 = ((bf16[8,128,256]{2,1,0:T(8,128)(2,1)}), bf16[8,128,256]{2,1,0:T(8,128)(2,1)S(1)}, u32[]{:S(2)}, u32[]{:S(2)}) async-start(bf16[8,128,256]{2,1,0:T(8,128)(2,1)} %combine.1), calls=%async_computation.2 | async-start | bytes 1048576 | tf_op jit(solution)/shard_map/all_to_all | solution.py:283
  86.0 5.6 %backward.1 = (bf16[3,2,128,256]{3,2,1,0:T(8,128)(2,1)}, bf16[3,2,128,256]{3,2,1,0:T(8,128)(2,1)}, bf16[3,2,128,256]{3,2,1,0:T(8,128)(2,1)}, bf16[4,256,128]{2,1,0:T(8,128)(2,1)}) custom-call(s32[2,6]{1,0:T(2,128)} %win_ref.3, bf16[4,2,128,256]{3,2,1,0:T(8,128)(2,1)} %copy-done.1, bf16[4,320,128]{2,1,0:T(8,128)(2,1)} %copy-done, ...), custom_call_target="tpu_custom_call" | custom-call | flops 1509949440 | bytes 1048576 | tf_op jit(solution)/shard_map/backward/pallas_call | solution.py:335
  91.6 4.7 %all-to-all-done.2.att_ref = bf16[8,128,256]{2,1,0:T(8,128)(2,1)S(1)} async-done(((bf16[8,128,256]{2,1,0:T(8,128)(2,1)}), bf16[8,128,256]{2,1,0:T(8,128)(2,1)S(1)}, u32[]{:S(2)}, u32[]{:S(2)}) %all-to-all-start.2) | async-done | bytes 524320 | tf_op jit(solution)/shard_map/all_to_all | solution.py:283
  96.9 18.4 %all_to_all.30.weight_ref = bf16[16,48,128]{2,1,0:T(8,128)(2,1)S(1)} all-to-all(bf16[16,48,128]{2,1,0:T(8,128)(2,1)S(1)} %weight.1), channel_id=1, replica_groups=mesh['tm'=4,'y'=4,'zh'=4,'x'=4,'core'=2] {'tm','y'}, dimensions={0} | all-to-all | bytes 393216 | tf_op jit(solution)/shard_map/all_to_all | solution.py:283
  116.1 4.0 %all-to-all-start.4 = ((bf16[4,304,128]{2,1,0:T(8,128)(2,1)}), bf16[4,304,128]{2,1,0:T(8,128)(2,1)S(1)}, u32[]{:S(2)}, u32[]{:S(2)}) async-start(bf16[4,304,128]{2,1,0:T(8,128)(2,1)} %merge.1), calls=%async_computation.4 | async-start | bytes 622592 | tf_op jit(solution)/shard_map/all_to_all | solution.py:283
  122.5 3.6 %collective-permute-start.9 = (bf16[3,2,128,256]{3,2,1,0:T(8,128)(2,1)S(1)}, bf16[3,2,128,256]{3,2,1,0:T(8,128)(2,1)S(1)}, u32[]{:S(2)}, u32[]{:S(2)}) collective-permute-start(bf16[3,2,128,256]{3,2,1,0:T(8,128)(2,1)S(1)} %copy-done.8), channel_id=1, source_target_pairs={{32,0},{64,32},{96,64},{33,1},{65,33},{97,65},{34,2},{66,34},{98,6... | collective-permute-start | bytes 1179656 | tf_op jit(solution)/shard_map/ppermute | solution.py:275
  126.0 4.9 %collective-permute-done.8.low_ref = bf16[3,2,128,256]{3,2,1,0:T(8,128)(2,1)S(1)} collective-permute-done((bf16[3,2,128,256]{3,2,1,0:T(8,128)(2,1)S(1)}, bf16[3,2,128,256]{3,2,1,0:T(8,128)(2,1)S(1)}, u32[]{:S(2)}, u32[]{:S(2)}) %collective-permute-start.8) | collective-permute-done | bytes 393248 | tf_op jit(solution)/shard_map/ppermute | solution.py:275
  132.9 6.9 %all-to-all-done.4.parts_ref = bf16[4,304,128]{2,1,0:T(8,128)(2,1)S(1)} async-done(((bf16[4,304,128]{2,1,0:T(8,128)(2,1)}), bf16[4,304,128]{2,1,0:T(8,128)(2,1)S(1)}, u32[]{:S(2)}, u32[]{:S(2)}) %all-to-all-start.4) | async-done | bytes 311328 | tf_op jit(solution)/shard_map/all_to_all | solution.py:283
  140.5 5.0 %all-to-all-start.5 = ((bf16[16,48,128]{2,1,0:T(8,128)(2,1)}), bf16[16,48,128]{2,1,0:T(8,128)(2,1)S(1)}, u32[]{:S(2)}, u32[]{:S(2)}) async-start(bf16[16,48,128]{2,1,0:T(8,128)(2,1)} %get-tuple-element.44), calls=%async_computation.5 | async-start | bytes 393216 | tf_op jit(solution)/shard_map/all_to_all | solution.py:283
  145.7 3.4 %collective-permute-start.10 = (bf16[2,128,256]{2,1,0:T(8,128)(2,1)S(1)}, bf16[2,128,256]{2,1,0:T(8,128)(2,1)S(1)}, u32[]{:S(2)}, u32[]{:S(2)}) collective-permute-start(bf16[2,128,256]{2,1,0:T(8,128)(2,1)S(1)} %get-tuple-element.42), channel_id=1, source_target_pairs={{0,128},{128,256},{256,384},{1,129},{129,257},{257,385},{2,130},{1... | collective-permute-start | bytes 393224 | tf_op jit(solution)/shard_map/ppermute | solution.py:275
  151.6 4.4 %collective-permute-done.11.high_ref = bf16[2,128,256]{2,1,0:T(8,128)(2,1)S(1)} collective-permute-done((bf16[2,128,256]{2,1,0:T(8,128)(2,1)S(1)}, bf16[2,128,256]{2,1,0:T(8,128)(2,1)S(1)}, u32[]{:S(2)}, u32[]{:S(2)}) %collective-permute-start.11) | collective-permute-done | bytes 131104 | tf_op jit(solution)/shard_map/ppermute | solution.py:275
  (48 shorter events, 18.4 us)
Async XLA Ops:
  1.5 9.1 %collective-permute-start.1 = (bf16[2,128,256]{2,1,0:T(8,128)(2,1)S(1)}, bf16[2,128,256]{2,1,0:T(8,128)(2,1)S(1)}, u32[]{:S(2)}, u32[]{:S(2)}) collective-permute-start(bf16[2,128,256]{2,1,0:T(8,128)(2,1)S(1)} %get-tuple-element.57), channel_id=1, source_target_pairs={{128,0},{256,128},{384,256},{129,1},{257,129},{385,257},{130,2},{2... | collective-permute-start | bytes 393224 | tf_op jit(solution)/shard_map/ppermute | solution.py:275
  2.8 7.8 %collective-permute-start = (bf16[2,128,256]{2,1,0:T(8,128)(2,1)S(1)}, bf16[2,128,256]{2,1,0:T(8,128)(2,1)S(1)}, u32[]{:S(2)}, u32[]{:S(2)}) collective-permute-start(bf16[2,128,256]{2,1,0:T(8,128)(2,1)S(1)} %get-tuple-element.57), channel_id=1, source_target_pairs={{0,128},{128,256},{256,384},{1,129},{129,257},{257,385},{2,130},{1... | collective-permute-start | bytes 393224 | tf_op jit(solution)/shard_map/ppermute | solution.py:275
  10.6 40.5 %all-to-all-start = ((bf16[4,2,128,256]{3,2,1,0:T(8,128)(2,1)}), bf16[4,2,128,256]{3,2,1,0:T(8,128)(2,1)S(1)}, u32[]{:S(2)}, u32[]{:S(2)}) async-start(bf16[4,2,128,256]{3,2,1,0:T(8,128)(2,1)} %get-tuple-element.27), calls=%async_computation | async-start | bytes 1048576 | tf_op jit(solution)/shard_map/all_to_all | solution.py:283
  25.7 25.4 %copy-start.7 = (s32[2,6]{1,0:T(2,128)S(1)}, s32[2,6]{1,0:T(2,128)}, u32[]{:S(2)}) copy-start(s32[2,6]{1,0:T(2,128)} %win_ref.3) | copy-start | bytes 148
  25.7 9.1 %collective-permute-start.4 = (bf16[4,128,384]{2,1,0:T(8,128)(2,1)}, bf16[4,128,384]{2,1,0:T(8,128)(2,1)S(1)}, u32[]{:S(2)}, u32[]{:S(2)}) collective-permute-start(bf16[4,128,384]{2,1,0:T(8,128)(2,1)} %get-tuple-element.31), channel_id=1, source_target_pairs={{0,1},{1,0},{2,3},{3,2},{4,5},{5,4},{6,7},{7,6},{8,9},{9,8},{10,11... | collective-permute-start | bytes 1179656 | tf_op jit(solution)/shard_map/ppermute | solution.py:316
  28.9 26.1 %copy-start.2 = (bf16[3,2,128,256]{3,2,1,0:T(8,128)(2,1)}, bf16[3,2,128,256]{3,2,1,0:T(8,128)(2,1)S(1)}, u32[]{:S(2)}) copy-start(bf16[3,2,128,256]{3,2,1,0:T(8,128)(2,1)S(1)} %pad_maximum_fusion.own_ref) | copy-start | bytes 1179652
  28.9 13.4 %collective-permute-start.3 = (bf16[3,2,128,256]{3,2,1,0:T(8,128)(2,1)S(1)}, bf16[3,2,128,256]{3,2,1,0:T(8,128)(2,1)S(1)}, u32[]{:S(2)}, u32[]{:S(2)}) collective-permute-start(bf16[3,2,128,256]{3,2,1,0:T(8,128)(2,1)S(1)} %pad_maximum_fusion.own_ref), channel_id=1, source_target_pairs={{32,0},{64,32},{96,64},{33,1},{65,33},{97,65},{34,2},{66,34},{98,6... | collective-permute-start | bytes 1179656 | tf_op jit(solution)/shard_map/ppermute | solution.py:275
  31.3 13.1 %collective-permute-start.2 = (bf16[3,2,128,256]{3,2,1,0:T(8,128)(2,1)S(1)}, bf16[3,2,128,256]{3,2,1,0:T(8,128)(2,1)S(1)}, u32[]{:S(2)}, u32[]{:S(2)}) collective-permute-start(bf16[3,2,128,256]{3,2,1,0:T(8,128)(2,1)S(1)} %pad_maximum_fusion.own_ref), channel_id=1, source_target_pairs={{0,32},{32,64},{64,96},{1,33},{33,65},{65,97},{2,34},{34,66},{66,9... | collective-permute-start | bytes 1179656 | tf_op jit(solution)/shard_map/ppermute | solution.py:275
  34.9 20.1 %collective-permute-start.5 = (bf16[2,128,384]{2,1,0:T(8,128)(2,1)S(1)}, bf16[2,128,384]{2,1,0:T(8,128)(2,1)S(1)}, u32[]{:S(2)}, u32[]{:S(2)}) collective-permute-start(bf16[2,128,384]{2,1,0:T(8,128)(2,1)S(1)} %pad_maximum_fusion.1), channel_id=1, source_target_pairs={{0,2},{2,4},{4,6},{6,0},{1,3},{3,5},{5,7},{7,1},{8,10},{10,12},{12... | collective-permute-start | bytes 589832 | tf_op jit(solution)/shard_map/ppermute | solution.py:320
  42.3 12.6 %copy-start.5 = (bf16[3,2,128,256]{3,2,1,0:T(8,128)(2,1)}, bf16[3,2,128,256]{3,2,1,0:T(8,128)(2,1)S(1)}, u32[]{:S(2)}) copy-start(bf16[3,2,128,256]{3,2,1,0:T(8,128)(2,1)S(1)} %collective-permute-done.3.high_ref) | copy-start | bytes 1179652
  55.0 25.8 %all-to-all-start.1 = ((bf16[4,320,128]{2,1,0:T(8,128)(2,1)}), bf16[4,320,128]{2,1,0:T(8,128)(2,1)S(1)}, u32[]{:S(2)}, u32[]{:S(2)}) async-start(bf16[4,320,128]{2,1,0:T(8,128)(2,1)} %forward.1), calls=%async_computation.1 | async-start | bytes 655360 | tf_op jit(solution)/shard_map/all_to_all | solution.py:283
  64.5 17.3 %collective-permute-start.6 = (bf16[2,128,384]{2,1,0:T(8,128)(2,1)S(1)}, bf16[2,128,384]{2,1,0:T(8,128)(2,1)S(1)}, u32[]{:S(2)}, u32[]{:S(2)}) collective-permute-start(bf16[2,128,384]{2,1,0:T(8,128)(2,1)S(1)} %pad_maximum_fusion.2), channel_id=1, source_target_pairs={{0,4},{2,6},{4,0},{6,2},{1,5},{3,7},{5,1},{7,3},{8,12},{10,14},{12... | collective-permute-start | bytes 589832 | tf_op jit(solution)/shard_map/ppermute | solution.py:320
  69.5 12.3 %collective-permute-start.7 = (bf16[2,128,384]{2,1,0:T(8,128)(2,1)S(1)}, bf16[2,128,384]{2,1,0:T(8,128)(2,1)S(1)}, u32[]{:S(2)}, u32[]{:S(2)}) collective-permute-start(bf16[2,128,384]{2,1,0:T(8,128)(2,1)S(1)} %pad_maximum_fusion.3), channel_id=1, source_target_pairs={{0,6},{2,0},{4,2},{6,4},{1,7},{3,1},{5,3},{7,5},{8,14},{10,8},{12,... | collective-permute-start | bytes 589832 | tf_op jit(solution)/shard_map/ppermute | solution.py:320
  81.8 14.5 %all-to-all-start.2 = ((bf16[8,128,256]{2,1,0:T(8,128)(2,1)}), bf16[8,128,256]{2,1,0:T(8,128)(2,1)S(1)}, u32[]{:S(2)}, u32[]{:S(2)}) async-start(bf16[8,128,256]{2,1,0:T(8,128)(2,1)} %combine.1), calls=%async_computation.2 | async-start | bytes 1048576 | tf_op jit(solution)/shard_map/all_to_all | solution.py:283
  91.6 23.8 %copy-start.4 = (bf16[4,256,128]{2,1,0:T(8,128)(2,1)S(1)}, bf16[4,256,128]{2,1,0:T(8,128)(2,1)}, u32[]{:S(2)}) copy-start(bf16[4,256,128]{2,1,0:T(8,128)(2,1)} %get-tuple-element.33.dq_ref) | copy-start | bytes 786436
  96.3 23.9 %copy-start.9 = (bf16[3,2,128,256]{3,2,1,0:T(8,128)(2,1)S(1)}, bf16[3,2,128,256]{3,2,1,0:T(8,128)(2,1)}, u32[]{:S(2)}) copy-start(bf16[3,2,128,256]{3,2,1,0:T(8,128)(2,1)} %get-tuple-element.37) | copy-start | bytes 1179652
  96.3 26.2 %copy-start.8 = (bf16[3,2,128,256]{3,2,1,0:T(8,128)(2,1)S(1)}, bf16[3,2,128,256]{3,2,1,0:T(8,128)(2,1)}, u32[]{:S(2)}) copy-start(bf16[3,2,128,256]{3,2,1,0:T(8,128)(2,1)} %get-tuple-element.35) | copy-start | bytes 1179652
  96.9 48.7 %copy-start.3 = (bf16[3,2,128,256]{3,2,1,0:T(8,128)(2,1)S(1)}, bf16[3,2,128,256]{3,2,1,0:T(8,128)(2,1)}, u32[]{:S(2)}) copy-start(bf16[3,2,128,256]{3,2,1,0:T(8,128)(2,1)} %get-tuple-element.40.own_ref) | copy-start | bytes 1179652
  116.1 23.7 %all-to-all-start.4 = ((bf16[4,304,128]{2,1,0:T(8,128)(2,1)}), bf16[4,304,128]{2,1,0:T(8,128)(2,1)S(1)}, u32[]{:S(2)}, u32[]{:S(2)}) async-start(bf16[4,304,128]{2,1,0:T(8,128)(2,1)} %merge.1), calls=%async_computation.4 | async-start | bytes 622592 | tf_op jit(solution)/shard_map/all_to_all | solution.py:283
  120.1 10.8 %collective-permute-start.8 = (bf16[3,2,128,256]{3,2,1,0:T(8,128)(2,1)S(1)}, bf16[3,2,128,256]{3,2,1,0:T(8,128)(2,1)S(1)}, u32[]{:S(2)}, u32[]{:S(2)}) collective-permute-start(bf16[3,2,128,256]{3,2,1,0:T(8,128)(2,1)S(1)} %copy-done.9), channel_id=1, source_target_pairs={{0,32},{32,64},{64,96},{1,33},{33,65},{65,97},{2,34},{34,66},{66,9... | collective-permute-start | bytes 1179656 | tf_op jit(solution)/shard_map/ppermute | solution.py:275
  122.5 10.5 %collective-permute-start.9 = (bf16[3,2,128,256]{3,2,1,0:T(8,128)(2,1)S(1)}, bf16[3,2,128,256]{3,2,1,0:T(8,128)(2,1)S(1)}, u32[]{:S(2)}, u32[]{:S(2)}) collective-permute-start(bf16[3,2,128,256]{3,2,1,0:T(8,128)(2,1)S(1)} %copy-done.8), channel_id=1, source_target_pairs={{32,0},{64,32},{96,64},{33,1},{65,33},{97,65},{34,2},{66,34},{98,6... | collective-permute-start | bytes 1179656 | tf_op jit(solution)/shard_map/ppermute | solution.py:275
  140.5 15.5 %all-to-all-start.5 = ((bf16[16,48,128]{2,1,0:T(8,128)(2,1)}), bf16[16,48,128]{2,1,0:T(8,128)(2,1)S(1)}, u32[]{:S(2)}, u32[]{:S(2)}) async-start(bf16[16,48,128]{2,1,0:T(8,128)(2,1)} %get-tuple-element.44), calls=%async_computation.5 | async-start | bytes 393216 | tf_op jit(solution)/shard_map/all_to_all | solution.py:283
  145.7 5.9 %collective-permute-start.10 = (bf16[2,128,256]{2,1,0:T(8,128)(2,1)S(1)}, bf16[2,128,256]{2,1,0:T(8,128)(2,1)S(1)}, u32[]{:S(2)}, u32[]{:S(2)}) collective-permute-start(bf16[2,128,256]{2,1,0:T(8,128)(2,1)S(1)} %get-tuple-element.42), channel_id=1, source_target_pairs={{0,128},{128,256},{256,384},{1,129},{129,257},{257,385},{2,130},{1... | collective-permute-start | bytes 393224 | tf_op jit(solution)/shard_map/ppermute | solution.py:275
  149.1 6.9 %collective-permute-start.11 = (bf16[2,128,256]{2,1,0:T(8,128)(2,1)S(1)}, bf16[2,128,256]{2,1,0:T(8,128)(2,1)S(1)}, u32[]{:S(2)}, u32[]{:S(2)}) collective-permute-start(bf16[2,128,256]{2,1,0:T(8,128)(2,1)S(1)} %get-tuple-element.43), channel_id=1, source_target_pairs={{128,0},{256,128},{384,256},{129,1},{257,129},{385,257},{130,2},{2... | collective-permute-start | bytes 393224 | tf_op jit(solution)/shard_map/ppermute | solution.py:275
  (3 other events, 19.6 us)
